TPU v7x, 32 devices: a whole 2x2x4 slice. The times are simulated.
32 devices in a mesh: ctx: 2 (over x), user: 16 (over z, y, core).
Axes of the slice: x: 2, y: 2, z: 4, core: 2. Of those that a mesh axis runs over, the one named last changes fastest.
Arguments:
- queries: bfloat16 [16, 512, 512], P('user', 'ctx'), may hold values from -6 to 6
- key_rows: bfloat16 [16, 512, 512], P('user', 'ctx'), may hold values from -6 to 6
- value_rows: bfloat16 [16, 512, 512], P('user', 'ctx'), may hold values from -6 to 6
- gate_rows: bfloat16 [16, 512, 512], P('user', 'ctx'), may hold values from -6 to 6
- item_emb: bfloat16 [16, 512, 1024], P('user', 'ctx'), may hold values from -0.1875 to 0.1875
- labels: int32 [16, 512], P('user', 'ctx'), may hold values 0 or 1
- propensity: float32 [16, 512], P('user', 'ctx'), may hold values from 0.05 to 1
- requests: int32 [16, 512], P('user', 'ctx'), may hold values from 0 to 63, never falling along the last dimension, each value on 1 to 16 neighbouring positions
- lengths: int32 [16], P('user'), may hold values from 1 to 512, as said below
- w_out: bfloat16 [512, 1024], P(None, 'ctx'), may hold values from -0.25 to 0.25
Outputs:
- grad_query: float32 [16, 512, 512], P('user', 'ctx')
- grad_key: float32 [16, 512, 512], P('user', 'ctx')
- grad_value: float32 [16, 512, 512], P('user', 'ctx')
- grad_gate: float32 [16, 512, 512], P('user', 'ctx')
- grad_w_out: float32 [512, 1024], P('ctx', 'user')
Inputs may be any that keep to these rules, and one draw needn't show every extreme that they name: `lengths`: every history has at least one live event and some history has all 512 events live. `requests`: request ids never fall along a history; a request spans at most 16 events.
All inputs are finite; a program needn't handle non-finite values. No bound on the sum of `labels` on one device may be relied on, other than what follows from the above.
Results may differ from a plain program's by a relative error of at most 0.0056.
Values may be sent and summed in bfloat16 or wider, within the bound.
A program may use at most 64 MiB of HBM per device.

v0:
```python
import math

import jax
import jax.numpy as jnp
from jax import lax
from jax.sharding import PartitionSpec as P

HEADS = 4
HEAD_DIM = 128
REQS = 64


norm_eps = 1e-06


def silu_slope(values):
    sigmoid_v = jax.nn.sigmoid(values)
    return sigmoid_v * (1.0 + values * (1.0 - sigmoid_v))


def split_heads(block):
    return block.reshape(block.shape[0], HEADS, HEAD_DIM)


def local(
    queries, key_rows, value_rows, gate_rows, item_emb, labels, propensity, requests, lengths, w_out
):
    row_count = queries.shape[1]
    feat_width = queries.shape[2]
    groups = lax.axis_size("ctx")
    seq_len = row_count * groups
    offset = lax.axis_index("ctx") * row_count
    score_factor = 1.0 / math.sqrt(HEAD_DIM)
    own_query = queries[0]
    own_key = key_rows[0]
    own_value = value_rows[0]
    query_h = split_heads(own_query)
    key_h = split_heads(own_key)
    value_h = split_heads(own_value)
    gate_f = gate_rows[0].astype(jnp.float32)
    hist_len = lengths[0]
    own_pos = offset + jnp.arange(row_count, dtype=jnp.int32)
    is_live = own_pos < hist_len
    key_piece = lax.all_gather(own_key, "ctx", axis=0, tiled=True)
    value_piece = lax.all_gather(own_value, "ctx", axis=0, tiled=True)
    piece_len = key_piece.shape[0]
    key_pos = jnp.arange(piece_len, dtype=jnp.int32)
    scores = (
        jnp.einsum(
            "qhd,khd->hqk", query_h, split_heads(key_piece), preferred_element_type=jnp.float32
        )
        * score_factor
    )
    allowed = (key_pos[None, :] <= own_pos[:, None]) & (key_pos[None, :] < hist_len)
    weights = (jnp.where(allowed[None], jax.nn.silu(scores), 0.0) / seq_len).astype(jnp.bfloat16)
    added = jnp.einsum(
        "hqk,khd->qhd", weights, split_heads(value_piece), preferred_element_type=jnp.float32
    )
    attended = added.reshape(row_count, feat_width)
    row_mean = jnp.mean(attended, axis=-1, keepdims=True)
    centered = attended - row_mean
    variance = jnp.mean(centered * centered, axis=-1, keepdims=True)
    inv_std = lax.rsqrt(variance + norm_eps)
    normed = centered * inv_std
    mixed_out = (normed * gate_f).astype(jnp.bfloat16)
    onehot = (requests[0][:, None] == jnp.arange(REQS, dtype=jnp.int32)[None, :]).astype(
        jnp.float32
    )
    live_f = is_live.astype(jnp.float32)
    inv_prop = jnp.where(is_live, 1.0 / propensity[0], 0.0)
    inv_sum, live_count = lax.psum(
        (jnp.sum(onehot * inv_prop[:, None], axis=0), jnp.sum(onehot * live_f[:, None], axis=0)),
        "ctx",
    )
    full_w = lax.all_gather(w_out, "ctx", axis=1, tiled=True)
    projected = jnp.dot(mixed_out, full_w, preferred_element_type=jnp.float32)
    item_f = item_emb[0].astype(jnp.float32)
    logits = jnp.sum(projected * item_f, axis=-1)
    ratio = jnp.where(live_count > 0, live_count / jnp.where(live_count > 0, inv_sum, 1.0), 0.0)
    event_weight = inv_prop * jnp.sum(onehot * ratio[None, :], axis=-1)
    grad_logits = event_weight * (jax.nn.sigmoid(logits) - labels[0].astype(jnp.float32))
    grad_proj = (grad_logits[:, None] * item_f).astype(jnp.bfloat16)
    whole_grad = lax.dot_general(
        mixed_out, grad_proj, (((0,), (0,)), ((), ())), preferred_element_type=jnp.float32
    )
    partial_grad = lax.psum_scatter(whole_grad, "user", scatter_dimension=1, tiled=True)
    grad_w = lax.psum_scatter(partial_grad, "ctx", scatter_dimension=0, tiled=True)
    grad_mixed = lax.dot_general(
        grad_proj, full_w, (((1,), (1,)), ((), ())), preferred_element_type=jnp.float32
    )
    grad_gate = grad_mixed * normed
    grad_normed = grad_mixed * gate_f
    grad_attn = (
        grad_normed
        - jnp.mean(grad_normed, axis=-1, keepdims=True)
        - normed * jnp.mean(grad_normed * normed, axis=-1, keepdims=True)
    ) * inv_std
    grad_attn = grad_attn.astype(jnp.bfloat16)
    grad_attn_h = split_heads(grad_attn)
    key_piece = lax.all_gather(own_key, "ctx", axis=0, tiled=True)
    value_piece = lax.all_gather(own_value, "ctx", axis=0, tiled=True)
    piece_len = key_piece.shape[0]
    key_pos = jnp.arange(piece_len, dtype=jnp.int32)
    key_piece_h = split_heads(key_piece)
    scores = (
        jnp.einsum("qhd,khd->hqk", query_h, key_piece_h, preferred_element_type=jnp.float32)
        * score_factor
    )
    allowed = (key_pos[None, :] <= own_pos[:, None]) & (key_pos[None, :] < hist_len)
    grad_weights = jnp.einsum(
        "qhd,khd->hqk", grad_attn_h, split_heads(value_piece), preferred_element_type=jnp.float32
    )
    grad_scores = (
        jnp.where(allowed[None], grad_weights * silu_slope(scores), 0.0) / seq_len
    ).astype(jnp.bfloat16)
    added = (
        jnp.einsum("hqk,khd->qhd", grad_scores, key_piece_h, preferred_element_type=jnp.float32)
        * score_factor
    )
    grad_query = added.reshape(row_count, feat_width)
    query_piece = lax.all_gather(own_query, "ctx", axis=0, tiled=True)
    grad_piece = lax.all_gather(grad_attn, "ctx", axis=0, tiled=True)
    piece_len = query_piece.shape[0]
    query_pos = jnp.arange(piece_len, dtype=jnp.int32)
    query_piece_h = split_heads(query_piece)
    grad_piece_h = split_heads(grad_piece)
    scores = (
        jnp.einsum("qhd,khd->hqk", query_piece_h, key_h, preferred_element_type=jnp.float32)
        * score_factor
    )
    allowed = (own_pos[None, :] <= query_pos[:, None]) & (own_pos[None, :] < hist_len)
    weights = (jnp.where(allowed[None], jax.nn.silu(scores), 0.0) / seq_len).astype(jnp.bfloat16)
    grad_weights = jnp.einsum(
        "qhd,khd->hqk", grad_piece_h, value_h, preferred_element_type=jnp.float32
    )
    grad_scores = (
        jnp.where(allowed[None], grad_weights * silu_slope(scores), 0.0) / seq_len
    ).astype(jnp.bfloat16)
    added_key = (
        jnp.einsum("hqk,qhd->khd", grad_scores, query_piece_h, preferred_element_type=jnp.float32)
        * score_factor
    )
    added_value = jnp.einsum(
        "hqk,qhd->khd", weights, grad_piece_h, preferred_element_type=jnp.float32
    )
    grad_key = added_key.reshape(row_count, feat_width)
    grad_value = added_value.reshape(row_count, feat_width)
    return (grad_query[None], grad_key[None], grad_value[None], grad_gate[None], grad_w)


def solution(mesh):
    in_specs = (
        P("user", "ctx", None),
        P("user", "ctx", None),
        P("user", "ctx", None),
        P("user", "ctx", None),
        P("user", "ctx", None),
        P("user", "ctx"),
        P("user", "ctx"),
        P("user", "ctx"),
        P("user"),
        P(None, "ctx"),
    )
    out_specs = (
        P("user", "ctx", None),
        P("user", "ctx", None),
        P("user", "ctx", None),
        P("user", "ctx", None),
        P("ctx", "user"),
    )
    return jax.shard_map(local, mesh=mesh, in_specs=in_specs, out_specs=out_specs, check_vma=False)
```

profile of v0, /device:TPU:0, one launch (start us, length us, event | category | flops | bytes accessed | tf_op | source)
XLA Modules:
  0.0 137.7 jit_solution(14118137255185259005)
XLA Ops:
  7.2 0.7 all-gather.5.cloned.1.call-update
  8.0 1.1 copy.39
  9.1 9.9 %all-gather = bf16[1,512,512]{1,2,0:T(8,128)(2,1)S(1)} all-gather(bf16[1,256,512]{1,2,0:T(8,128)(2,1)S(1)} %copy.39), channel_id=2, replica_groups=mesh['ctx'=2,'user'=16] {'ctx'}, dimensions={1}, use_global_device_ids=true | all-gather | bytes 786432 | tf_op jit(solution)/shard_map/all_gather | solution.py:100
  19.0 1.2 reshape_squeeze.9
  20.2 14.8 %all-gather.1 = bf16[1,512,512]{2,1,0:T(8,128)(2,1)S(1)} all-gather(bf16[1,256,512]{2,1,0:T(8,128)(2,1)S(1)} %copy-done.6), channel_id=3, replica_groups=mesh['ctx'=2,'user'=16] {'ctx'}, dimensions={1}, use_global_device_ids=true | all-gather | bytes 786432 | tf_op jit(solution)/shard_map/all_gather | solution.py:45
  34.9 1.0 copy.42
  37.4 4.9 %all-reduce = (f32[64]{0:T(128)S(1)}, f32[64]{0:T(128)S(1)}) all-reduce(f32[64]{0:T(128)S(1)} %get-tuple-element.23, f32[64]{0:T(128)S(1)} %get-tuple-element.22), channel_id=1, replica_groups=mesh['ctx'=2,'user'=16] {'ctx'}, use_global_device_ids=true, to_apply=%region_1.2 | all-reduce | flops 128 | bytes 1024 | tf_op jit(solution)/shard_map/psum | solution.py:71
  42.3 2.6 %fusion.64 = (f32[256]{0:T(256)}, f32[4,256,128]{1,2,0:T(8,128)S(1)}) fusion(bf16[512,4,128]{0,2,1:T(8,128)(2,1)} %bitcast.86, f32[4,256,512]{2,1,0:T(8,128)S(1)} %fusion.39, pred[256,512]{1,0:T(8,128)(4,1)S(1)} %fusion.28), kind=kOutput, calls=%fused_computation.94 | convolution fusion | flops 138542848 | bytes 3277824 | tf_op jit(solution)/shard_map/hqk,khd->qhd/dot_general | solution.py:56
  44.9 1.0 copy.43
  46.5 1.1 copy.52
  47.6 0.7 select_reduce_fusion
  48.2 0.7 broadcast_multiply_fusion.2
  49.0 0.8 multiply_convert_fusion.6
  49.8 2.2 %fusion.3 = f32[256]{0:T(256)S(1)} fusion(bf16[1,256,1024]{2,1,0:T(8,128)(2,1)} %param.14, bf16[512,1024]{1,0:T(8,128)(2,1)} %all-gather.5.cloned.1.call-done, f32[256,512]{1,0:T(8,128)} %copy.43, bf16[1,256,512]{2,1,0:T(8,128)(2,1)} %param.13, f32[256]{0:T(256)S(1)} %add_rsqrt_fusion, f32[256]{0:T(256)S(1)} %broadcast_multiply_fusion.2), kind=kOutput, calls=%fused_computation.12 | convolution fusion | flops 269876992 | bytes 2362368 | tf_op jit(solution)/shard_map/dot_general | solution.py:76
  52.1 0.7 fusion.45
  52.8 3.0 %fusion.21 = f32[512,1024]{0,1:T(8,128)} fusion(bf16[256,512]{0,1:T(8,128)(2,1)S(1)} %bitcast.85, bf16[1,256,1024]{2,1,0:T(8,128)(2,1)} %param.14, f32[256]{0:T(256)S(1)} %fusion.45), kind=kOutput, calls=%fused_computation.30 | convolution fusion | flops 269221888 | bytes 2884608 | tf_op jit(solution)/shard_map/dot_general | solution.py:83
  56.1 0.8 reshape_squeeze.10
  56.9 7.2 %all-gather.2 = bf16[1,512,512]{1,2,0:T(8,128)(2,1)S(1)} all-gather(bf16[1,256,512]{1,2,0:T(8,128)(2,1)S(1)} %copy.48), channel_id=4, replica_groups=mesh['ctx'=2,'user'=16] {'ctx'}, dimensions={1}, use_global_device_ids=true | all-gather | bytes 786432 | tf_op jit(solution)/shard_map/all_gather | solution.py:121
  64.1 0.8 fusion.29
  64.9 1.8 %fusion.35 = f32[4,512,256]{2,1,0:T(8,128)} fusion(bf16[512,4,128]{0,2,1:T(8,128)(2,1)S(1)} %bitcast.83, bf16[256,4,128]{2,1,0:T(4,128)(2,1)S(1)} %reshape_squeeze.11), kind=kOutput, calls=%fused_computation.50 | convolution fusion | flops 134217728 | bytes 2883584 | tf_op jit(solution)/shard_map/qhd,khd->hqk/dot_general | solution.py:128
  66.7 0.6 fusion.44
  67.4 1.1 multiply_bitcast_fusion
  68.5 3.4 %fusion.4 = f32[4,256,128]{1,2,0:T(8,128)} fusion(bf16[512,4,128]{0,2,1:T(8,128)(2,1)S(1)} %bitcast.82, f32[4,256,512]{2,1,0:T(8,128)S(1)} %fusion.39, bf16[512,4,128]{0,2,1:T(8,128)(2,1)} %bitcast.87, pred[256,512]{1,0:T(8,128)(4,1)S(1)} %fusion.28, bf16[256,512]{1,0:T(8,128)(2,1)} %get-tuple-element.29), kind=kOutput, calls=%fused_computation.13 | convolution fusion | flops 274857984 | bytes 4063232 | tf_op jit(solution)/shard_map/hqk,khd->qhd/dot_general | solution.py:117
  71.9 2.2 %copy.53 = f32[1,256,512]{2,1,0:T(8,128)} copy(f32[1,256,512]{1,2,0:T(8,128)} %bitcast.90) | data formatting | bytes 1048576
  74.1 7.0 %all_gather.20 = bf16[512,512]{1,0:T(8,128)(2,1)S(1)} all-gather(bf16[256,512]{1,0:T(8,128)(2,1)S(1)} %copy-done.10), channel_id=1, replica_groups=mesh['ctx'=2,'user'=16] {'ctx'}, dimensions={0}, use_global_device_ids=true | all-gather | bytes 786432 | tf_op jit(solution)/shard_map/all_gather | solution.py:122
  81.1 1.0 copy.59
  82.1 3.4 %fusion.5 = f32[4,256,128]{1,2,0:T(8,128)} fusion(bf16[512,4,128]{0,2,1:T(8,128)(2,1)S(1)} %bitcast.84, f32[4,512,256]{2,1,0:T(8,128)S(1)} %copy-done, bf16[512,4,128]{0,2,1:T(8,128)(2,1)} %bitcast.88, pred[512,256]{1,0:T(8,128)(4,1)S(1)} %copy-done.14, bf16[256,4,128]{2,1,0:T(4,128)(2,1)} %reshape_squeeze.10), kind=kOutput, calls=%fused_computation.14 | convolution fusion | flops 274857984 | bytes 4063232 | tf_op jit(solution)/shard_map/hqk,qhd->khd/dot_general | solution.py:140
  85.5 2.0 %copy.54 = f32[1,256,512]{2,1,0:T(8,128)} copy(f32[1,256,512]{1,2,0:T(8,128)} %bitcast.92) | data formatting | bytes 1048576
  87.6 31.5 %reduce-scatter.3.cloned.1.call-done = f32[512,64]{0,1:T(8,128)} async-done(((f32[512,1024]{0,1:T(8,128)}), f32[512,64]{0,1:T(8,128)}) %reduce-scatter.3.cloned.1.call-update) | async-done | bytes 131088 | tf_op jit(solution)/shard_map/reduce_scatter | solution.py:86
  119.1 0.9 fusion.19
  120.0 1.0 copy.55
  121.0 10.2 %reduce-scatter.5.cloned.1.call-done = f32[256,64]{0,1:T(8,128)} async-done(((f32[512,64]{0,1:T(8,128)}), f32[256,64]{0,1:T(8,128)}) %reduce-scatter.5.cloned.1.call-update) | async-done | bytes 65552 | tf_op jit(solution)/shard_map/reduce_scatter | solution.py:87
  (69 shorter events, 1.9 us)
Async XLA Ops:
  7.2 13.0 %copy-start.6 = (bf16[1,256,512]{2,1,0:T(8,128)(2,1)S(1)}, bf16[1,256,512]{2,1,0:T(8,128)(2,1)}, u32[]{:S(2)}) copy-start(bf16[1,256,512]{2,1,0:T(8,128)(2,1)} %param.12) | copy-start | bytes 786436
  7.2 29.5 %copy-start.21 = (f32[1,256]{1,0:T(1,128)S(1)}, f32[1,256]{1,0:T(1,128)}, u32[]{:S(2)}) copy-start(f32[1,256]{1,0:T(1,128)} %param.16) | copy-start | bytes 3076
  7.2 42.6 %all-gather.5.cloned.1.call-start = ((), (), s32[]{:S(2)}) async-start(), calls=%async_computation.2 | async-start | bytes 1572864 | tf_op jit(solution)/shard_map/all_gather | solution.py:75
  7.9 111.1 %reduce-scatter.3.cloned.1.call-start = ((), (), s32[]{:S(2)}) async-start(), calls=%async_computation.3 | async-start | bytes 2228224 | tf_op jit(solution)/shard_map/reduce_scatter | solution.py:86
  19.0 18.1 %copy-start.1 = (bf16[1,512,512]{1,2,0:T(8,128)(2,1)}, bf16[1,512,512]{1,2,0:T(8,128)(2,1)S(1)}, u32[]{:S(2)}) copy-start(bf16[1,512,512]{1,2,0:T(8,128)(2,1)S(1)} %all-gather) | copy-start | bytes 1572868
  34.9 2.3 %copy-start.19 = (s32[1,256]{1,0:T(1,128)S(1)}, s32[1,256]{1,0:T(1,128)}, u32[]{:S(2)}) copy-start(s32[1,256]{1,0:T(1,128)} %param.17) | copy-start | bytes 3076
  35.9 9.0 %copy-start.15 = (s32[256]{0:T(256)}, s32[256]{0:T(256)S(1)}, u32[]{:S(2)}) copy-start(s32[256]{0:T(256)S(1)} %iota_add_fusion) | copy-start | bytes 3076
  42.3 3.6 %copy-start.22 = (s32[1,256]{1,0:T(1,128)S(1)}, s32[1,256]{1,0:T(1,128)}, u32[]{:S(2)}) copy-start(s32[1,256]{1,0:T(1,128)} %param.15) | copy-start | bytes 3076
  42.3 5.3 %copy-start.20 = (s32[1,256]{1,0:T(1,128)S(1)}, s32[1,256]{1,0:T(1,128)}, u32[]{:S(2)}) copy-start(s32[1,256]{1,0:T(1,128)} %param.17) | copy-start | bytes 3076
  49.8 2.9 %copy-start.11 = (bf16[256,4,128]{0,2,1:T(8,128)(2,1)S(1)}, bf16[256,4,128]{0,2,1:T(8,128)(2,1)}, u32[]{:S(2)}) copy-start(bf16[256,4,128]{0,2,1:T(8,128)(2,1)} %multiply_convert_fusion.6) | copy-start | bytes 786436
  52.7 3.1 %copy-start.17 = (f32[256]{0:T(256)}, f32[256]{0:T(256)S(1)}, u32[]{:S(2)}) copy-start(f32[256]{0:T(256)S(1)} %fusion.45) | copy-start | bytes 3076
  52.7 3.1 %copy-start.7 = (bf16[1,256,512]{2,1,0:T(8,128)(2,1)S(1)}, bf16[1,256,512]{2,1,0:T(8,128)(2,1)}, u32[]{:S(2)}) copy-start(bf16[1,256,512]{2,1,0:T(8,128)(2,1)} %param.10) | copy-start | bytes 786436
  52.8 3.3 %copy-start.8 = (bf16[1,256,512]{2,1,0:T(8,128)(2,1)S(1)}, bf16[1,256,512]{2,1,0:T(8,128)(2,1)}, u32[]{:S(2)}) copy-start(bf16[1,256,512]{2,1,0:T(8,128)(2,1)} %param.11) | copy-start | bytes 786436
  55.8 8.3 %copy-start.16 = (s32[256]{0:T(256)S(1)}, s32[256]{0:T(256)}, u32[]{:S(2)}) copy-start(s32[256]{0:T(256)} %copy-done.15) | copy-start | bytes 3076
  55.8 75.4 %reduce-scatter.5.cloned.1.call-start = ((), (), s32[]{:S(2)}) async-start(), calls=%async_computation.4 | async-start | bytes 196608 | tf_op jit(solution)/shard_map/reduce_scatter | solution.py:87
  56.1 10.6 %copy-start.3 = (f32[256,512]{1,0:T(8,128)S(1)}, f32[256,512]{1,0:T(8,128)}, u32[]{:S(2)}) copy-start(f32[256,512]{1,0:T(8,128)} %copy.43) | copy-start | bytes 1572868
  56.9 9.8 %copy-start.9 = (bf16[1,256,512]{2,1,0:T(8,128)(2,1)S(1)}, bf16[1,256,512]{2,1,0:T(8,128)(2,1)}, u32[]{:S(2)}) copy-start(bf16[1,256,512]{2,1,0:T(8,128)(2,1)} %param.13) | copy-start | bytes 786436
  56.9 9.8 %copy-start.13 = (bf16[1,256,1024]{2,1,0:T(8,128)(2,1)S(1)}, bf16[1,256,1024]{2,1,0:T(8,128)(2,1)}, u32[]{:S(2)}) copy-start(bf16[1,256,1024]{2,1,0:T(8,128)(2,1)} %param.14) | copy-start | bytes 1572868
  56.9 9.8 %copy-start.18 = (f32[256]{0:T(256)S(1)}, f32[256]{0:T(256)}, u32[]{:S(2)}) copy-start(f32[256]{0:T(256)} %copy-done.17) | copy-start | bytes 3076
  56.9 9.8 %copy-start.23 = (bf16[512,1024]{1,0:T(8,128)(2,1)S(1)}, bf16[512,1024]{1,0:T(8,128)(2,1)}, u32[]{:S(2)}) copy-start(bf16[512,1024]{1,0:T(8,128)(2,1)} %all-gather.5.cloned.1.call-done) | copy-start | bytes 3145732
  64.0 0.8 copy-start.4
  66.7 1.8 %copy-start.2 = (bf16[1,512,512]{1,2,0:T(8,128)(2,1)S(1)}, bf16[1,512,512]{1,2,0:T(8,128)(2,1)}, u32[]{:S(2)}) copy-start(bf16[1,512,512]{1,2,0:T(8,128)(2,1)} %copy-done.1) | copy-start | bytes 1572868
  68.5 5.6 %copy-start.10 = (bf16[256,512]{1,0:T(8,128)(2,1)S(1)}, bf16[256,512]{1,0:T(8,128)(2,1)}, u32[]{:S(2)}) copy-start(bf16[256,512]{1,0:T(8,128)(2,1)} %get-tuple-element.29) | copy-start | bytes 786436
  71.9 10.3 %copy-start = (f32[4,512,256]{2,1,0:T(8,128)S(1)}, f32[4,512,256]{2,1,0:T(8,128)}, u32[]{:S(2)}) copy-start(f32[4,512,256]{2,1,0:T(8,128)} %fusion.35) | copy-start | bytes 6291460
  71.9 10.3 %copy-start.5 = (bf16[1,512,512]{1,2,0:T(8,128)(2,1)S(1)}, bf16[1,512,512]{1,2,0:T(8,128)(2,1)}, u32[]{:S(2)}) copy-start(bf16[1,512,512]{1,2,0:T(8,128)(2,1)} %copy-done.4) | copy-start | bytes 1572868
  71.9 10.3 %copy-start.14 = (pred[512,256]{1,0:T(8,128)(4,1)S(1)}, pred[512,256]{1,0:T(8,128)(4,1)}, u32[]{:S(2)}) copy-start(pred[512,256]{1,0:T(8,128)(4,1)} %fusion.29) | copy-start | bytes 393220
  82.1 36.9 %copy-start.12 = (bf16[512,512]{0,1:T(8,128)(2,1)S(1)}, bf16[512,512]{0,1:T(8,128)(2,1)}, u32[]{:S(2)}) copy-start(bf16[512,512]{0,1:T(8,128)(2,1)} %copy.59) | copy-start | bytes 1572868
Sparse Core Ops, SparseCore 0:
  9.6 29.6 all-gather.4
  55.9 63.0 reduce-scatter.2
  121.9 9.2 reduce-scatter.4
where the time goes:
time: 138 us
  blocking collectives  43.8 us (32%)
  waiting for transfers between devices  42.4 us (31%)
  matrix products  18.3 us (13%)
  between operations  14.7 us (11%)
  local copies, waits for them, and re-layouts  12.7 us (9%)
  other arithmetic  5.75 us (4%)
    reduce_scatter x1, waiting for transfers between devices, local(): lax.psum_scatter(whole_grad, 'user', scatter_dimension=1, tiled=True)  31.5 us
    all_gather x1, blocking collectives, local(): value_piece = lax.all_gather(own_value, 'ctx', axis=0, tiled=True)  14.8 us
    reduce_scatter x1, waiting for transfers between devices, local(): lax.psum_scatter(partial_grad, 'ctx', scatter_dimension=0, tiled=True)  10.2 us
    all_gather x1, blocking collectives, local(): key_piece = lax.all_gather(own_key, 'ctx', axis=0, tiled=True)  9.91 us
    all_gather x1, blocking collectives, local(): query_piece = lax.all_gather(own_query, 'ctx', axis=0, tiled=True)  7.18 us
    all_gather x1, blocking collectives, local(): grad_piece = lax.all_gather(grad_attn, 'ctx', axis=0, tiled=True)  7.04 us
    unnamed x53, local copies, waits for them, and re-layouts  6.56 us
    psum x1, blocking collectives, local(): lax.psum((jnp.sum(onehot * inv_prop[:, None], axis=0), jnp.sum(onehot * l...  4.94 us
  transfers between devices with their start and end apart: 3, of which 2 were waited for; matrix products, arithmetic and copies ran while one was open for 22% of the time, Pallas kernels for 0%

commit v1 on v0

--- a/solution.py
+++ b/solution.py
@@ -1,8 +1,11 @@
+import functools
 import math
 
 import jax
 import jax.numpy as jnp
 from jax import lax
+from jax.experimental import pallas as pl
+from jax.experimental.pallas import tpu as pltpu
 from jax.sharding import PartitionSpec as P
 
 HEADS = 4
@@ -73,9 +76,11 @@
         "ctx",
     )
     full_w = lax.all_gather(w_out, "ctx", axis=1, tiled=True)
-    projected = jnp.dot(mixed_out, full_w, preferred_element_type=jnp.float32)
     item_f = item_emb[0].astype(jnp.float32)
-    logits = jnp.sum(projected * item_f, axis=-1)
+    item_proj = lax.dot_general(
+        item_emb[0], full_w, (((1,), (1,)), ((), ())), preferred_element_type=jnp.float32
+    )
+    logits = jnp.sum(mixed_out.astype(jnp.float32) * item_proj, axis=-1)
     ratio = jnp.where(live_count > 0, live_count / jnp.where(live_count > 0, inv_sum, 1.0), 0.0)
     event_weight = inv_prop * jnp.sum(onehot * ratio[None, :], axis=-1)
     grad_logits = event_weight * (jax.nn.sigmoid(logits) - labels[0].astype(jnp.float32))
@@ -85,9 +90,7 @@
     )
     partial_grad = lax.psum_scatter(whole_grad, "user", scatter_dimension=1, tiled=True)
     grad_w = lax.psum_scatter(partial_grad, "ctx", scatter_dimension=0, tiled=True)
-    grad_mixed = lax.dot_general(
-        grad_proj, full_w, (((1,), (1,)), ((), ())), preferred_element_type=jnp.float32
-    )
+    grad_mixed = grad_logits[:, None] * item_proj
     grad_gate = grad_mixed * normed
     grad_normed = grad_mixed * gate_f
     grad_attn = (
@@ -148,6 +151,361 @@
     return (grad_query[None], grad_key[None], grad_value[None], grad_gate[None], grad_w)
 
 
+MESH = pl.DeviceIdType.MESH
+F32 = jnp.float32
+BF16 = jnp.bfloat16
+
+
+def dot_nn(a, b):
+    return lax.dot_general(a, b, (((1,), (0,)), ((), ())), preferred_element_type=F32)
+
+
+def dot_nt(a, b):
+    return lax.dot_general(a, b, (((1,), (1,)), ((), ())), preferred_element_type=F32)
+
+
+def dot_tn(a, b):
+    return lax.dot_general(a, b, (((0,), (0,)), ((), ())), preferred_element_type=F32)
+
+
+def sigmoid(values):
+    return 0.5 * jnp.tanh(0.5 * values) + 0.5
+
+
+def head(h):
+    return slice(h * HEAD_DIM, (h + 1) * HEAD_DIM)
+
+
+def fused_kernel(
+    users,
+    len_ref, q_ref, k_ref, v_ref, gate_ref, item_ref, lab_ref, prop_ref, req_ref, w_ref,
+    dq_ref, dk_ref, dv_ref, dgate_ref, dw_ref,
+    ok, ov, oq, oda, wbuf, stat_out, stat_in,
+    wt, sl, wt_x, sl_x, att, u, da, gw,
+    r_core, s_y, r_y, s_z, r_z, fin, s_x, r_x,
+    ks, kr, vs, vr, qs, qr, das, dar, wss, wsr, sts, str_, cs, cr, ys, yr, zs, zr, xs, xr,
+):
+    rows, feats = q_ref.shape
+    width = item_ref.shape[1]
+    half_w = width // 2
+    seq_len = 2 * rows
+    nz = users // 4
+    cols = feats // 2
+    factor = 1.0 / math.sqrt(HEAD_DIM)
+    ctx = lax.axis_index("ctx")
+    user = lax.axis_index("user")
+    core = lax.rem(user, 2)
+    yy = lax.rem(lax.div(user, 2), 2)
+    zz = lax.div(user, 4)
+    quarter = lax.rem(user, 4)
+    offset = ctx * rows
+    x_peer = (1 - ctx, user)
+    c_peer = (ctx, user + 1 - 2 * core)
+    y_peer = (ctx, user + 2 - 4 * yy)
+    d_peer = (ctx, user + 3 - 2 * core - 4 * yy)
+    z_peers = [(ctx, quarter + 4 * lax.rem(zz + step, nz)) for step in range(1, nz)]
+
+    def remote(source, target, send_sem, recv_sem, device):
+        return pltpu.make_async_remote_copy(
+            src_ref=source, dst_ref=target, send_sem=send_sem, recv_sem=recv_sem,
+            device_id=device, device_id_type=MESH,
+        )
+
+    hist_len = len_ref[0]
+    reqs = req_ref[...]
+    onehot = (lax.broadcasted_iota(jnp.int32, (REQS, rows), 0) == reqs).astype(F32)
+    live = offset + lax.broadcasted_iota(jnp.int32, (1, rows), 1) < hist_len
+    inv_prop = jnp.where(live, 1.0 / prop_ref[...], 0.0)
+    own_inv = jnp.sum(onehot * inv_prop, axis=1, keepdims=True)
+    own_live = jnp.sum(onehot * jnp.where(live, 1.0, 0.0), axis=1, keepdims=True)
+    lane = lax.broadcasted_iota(jnp.int32, (REQS, 128), 1)
+    stat_out[...] = jnp.where(lane == 0, own_inv, own_live)
+
+    peers = [x_peer, c_peer, y_peer, d_peer] + z_peers
+    barrier = pltpu.get_barrier_semaphore()
+    for peer in peers:
+        pl.semaphore_signal(barrier, inc=1, device_id=peer, device_id_type=MESH)
+    pl.semaphore_wait(barrier, len(peers))
+
+    stat_copy = remote(stat_out, stat_in, sts, str_, x_peer)
+    w_part = feats // 4
+    w_rows = pl.ds(pl.multiple_of(quarter * w_part, w_part), w_part)
+    w_copy = remote(w_ref.at[w_rows], wbuf.at[quarter], wss.at[0], wsr.at[0], x_peer)
+    w_spread = [
+        remote(wbuf.at[quarter], wbuf.at[quarter], wss.at[i], wsr.at[i], peer)
+        for i, peer in ((1, c_peer), (2, y_peer), (3, d_peer))
+    ]
+    k_copy = [remote(k_ref.at[:, head(h)], ok.at[h], ks.at[h], kr.at[h], x_peer) for h in range(HEADS)]
+    v_copy = [remote(v_ref.at[:, head(h)], ov.at[h], vs.at[h], vr.at[h], x_peer) for h in range(HEADS)]
+    q_copy = [remote(q_ref.at[:, head(h)], oq.at[h], qs.at[h], qr.at[h], x_peer) for h in range(HEADS)]
+    da_copy = [remote(da.at[h], oda.at[h], das.at[h], dar.at[h], x_peer) for h in range(HEADS)]
+
+    stat_copy.start()
+    w_copy.start()
+
+    @pl.when(ctx == 0)
+    def _():
+        for h in range(HEADS):
+            k_copy[h].start()
+            v_copy[h].start()
+
+    @pl.when(ctx == 1)
+    def _():
+        for h in range(HEADS):
+            q_copy[h].start()
+
+    def gates(scores, allowed):
+        s = scores * factor
+        sig = sigmoid(s)
+        weight = jnp.where(allowed, s * sig, 0.0) * (1.0 / seq_len)
+        slope = jnp.where(allowed, sig * (1.0 + s * (1.0 - sig)), 0.0) * (1.0 / seq_len)
+        return weight.astype(BF16), slope
+
+    row_i = lax.broadcasted_iota(jnp.int32, (rows, rows), 0)
+    col_i = lax.broadcasted_iota(jnp.int32, (rows, rows), 1)
+    allowed = (col_i <= row_i) & (offset + col_i < hist_len)
+    for h in range(HEADS):
+        weight, slope = gates(dot_nt(q_ref[:, head(h)], k_ref[:, head(h)]), allowed)
+        wt[h] = weight
+        sl[h] = slope
+        att[:, head(h)] = dot_nn(weight, v_ref[:, head(h)])
+
+    own_cols = pl.ds(pl.multiple_of(ctx * half_w, half_w), half_w)
+    other_cols = pl.ds(pl.multiple_of((1 - ctx) * half_w, half_w), half_w)
+    w_copy.wait_recv()
+    for copy in w_spread:
+        copy.start()
+    u[...] = dot_nt(item_ref[:, own_cols], w_ref[...])
+
+    @pl.when(ctx == 1)
+    def _():
+        seen = lax.broadcasted_iota(jnp.int32, (rows, rows), 1) < hist_len
+        for h in range(HEADS):
+            k_copy[h].wait_recv()
+            weight, slope = gates(dot_nt(q_ref[:, head(h)], ok[h]), seen)
+            sl_x[h] = slope
+            v_copy[h].wait_recv()
+            att[:, head(h)] += dot_nn(weight, ov[h])
+
+    for copy in w_spread:
+        copy.wait_recv()
+    for part in range(4):
+        part_cols = slice(part * w_part, (part + 1) * w_part)
+        u[:, part_cols] += dot_nt(item_ref[:, other_cols], wbuf[part])
+
+    attended = att[...]
+    centered = attended - jnp.mean(attended, axis=-1, keepdims=True)
+    inv_std = lax.rsqrt(jnp.mean(centered * centered, axis=-1, keepdims=True) + norm_eps)
+    normed = centered * inv_std
+    gate_f = gate_ref[...].astype(F32)
+    mixed_out = (normed * gate_f).astype(BF16)
+    item_proj = u[...]
+    logits = jnp.sum(mixed_out.astype(F32) * item_proj, axis=-1, keepdims=True)
+
+    stat_copy.wait_recv()
+    both = stat_out[...] + stat_in[...]
+    inv_sum, live_count = both[:, 0:1], both[:, 1:2]
+    some = live_count > 0
+    ratio = jnp.where(some, live_count / jnp.where(some, inv_sum, 1.0), 0.0)
+    event_weight = inv_prop * jnp.sum(onehot * ratio, axis=0, keepdims=True)
+    eye = row_i == col_i
+    weight_col = jnp.sum(jnp.where(eye, event_weight, 0.0), axis=1, keepdims=True)
+    label_col = jnp.sum(jnp.where(eye, lab_ref[...].astype(F32), 0.0), axis=1, keepdims=True)
+    grad_logits = weight_col * (jax.nn.sigmoid(logits) - label_col)
+    grad_mixed = grad_logits * item_proj
+    dgate_ref[...] = grad_mixed * normed
+    grad_normed = grad_mixed * gate_f
+    grad_attn = (
+        grad_normed
+        - jnp.mean(grad_normed, axis=-1, keepdims=True)
+        - normed * jnp.mean(grad_normed * normed, axis=-1, keepdims=True)
+    ) * inv_std
+    for h in range(HEADS):
+        da[h] = grad_attn[:, head(h)].astype(BF16)
+
+    @pl.when(ctx == 1)
+    def _():
+        for h in range(HEADS):
+            da_copy[h].start()
+
+    per_user = width // users
+    for j in range(users // 2):
+        chunk_cols = slice(j * 2 * per_user, (j + 1) * 2 * per_user)
+        grad_proj = (grad_logits * item_ref[:, chunk_cols].astype(F32)).astype(BF16)
+        chunk = dot_tn(grad_proj, mixed_out).astype(BF16)
+        for c in range(2):
+            for half in range(2):
+                gw[c, half, j % 2, j // 2] = chunk[
+                    c * per_user : (c + 1) * per_user, half * cols : (half + 1) * cols
+                ]
+    halves = [1 - ctx, ctx]
+    c_copy = [remote(gw.at[1 - core, halves[o]], r_core.at[o], cs.at[o], cr.at[o], c_peer) for o in range(2)]
+    y_copy = [remote(s_y.at[o], r_y.at[o], ys.at[o], yr.at[o], y_peer) for o in range(2)]
+    z_copy = [
+        [
+            remote(
+                s_z.at[o, lax.rem(zz + i + 1, nz)], r_z.at[o, i], zs.at[o, i], zr.at[o, i], z_peers[i]
+            )
+            for i in range(nz - 1)
+        ]
+        for o in range(2)
+    ]
+    x_copy = remote(s_x, r_x, xs, xr, x_peer)
+    for o in range(2):
+        c_copy[o].start()
+
+    def after_core(o):
+        c_copy[o].wait_recv()
+        s_y[o] = (gw[core, halves[o], 1 - yy].astype(F32) + r_core[o, 1 - yy].astype(F32)).astype(BF16)
+        y_copy[o].start()
+
+    def after_y(o):
+        y_copy[o].wait_recv()
+        mine = gw[core, halves[o], yy].astype(F32) + r_core[o, yy].astype(F32)
+        s_z[o] = (mine + r_y[o].astype(F32)).astype(BF16)
+        for copy in z_copy[o]:
+            copy.start()
+
+    def after_z(o):
+        total = gw[core, halves[o], yy, zz].astype(F32) + r_core[o, yy, zz].astype(F32)
+        total += r_y[o, zz].astype(F32)
+        for i in range(nz - 1):
+            z_copy[o][i].wait_recv()
+            total += r_z[o, i].astype(F32)
+        if o == 0:
+            s_x[...] = total.astype(BF16)
+            x_copy.start()
+        else:
+            fin[...] = total
+
+    def backward(h):
+        grad_scores = (dot_nt(da[h], v_ref[:, head(h)]) * sl[h]).astype(BF16)
+        dq_ref[:, head(h)] = dot_nn(grad_scores, k_ref[:, head(h)]) * factor
+        dk_ref[:, head(h)] = dot_tn(grad_scores, q_ref[:, head(h)]) * factor
+        dv_ref[:, head(h)] = dot_tn(wt[h], da[h])
+
+    def cross_query(h):
+        grad_scores = (dot_nt(da[h], ov[h]) * sl_x[h]).astype(BF16)
+        dq_ref[:, head(h)] += dot_nn(grad_scores, ok[h]) * factor
+
+    def cross_scores(h):
+        q_copy[h].wait_recv()
+        seen = lax.broadcasted_iota(jnp.int32, (rows, rows), 1) < hist_len
+        weight, slope = gates(dot_nt(oq[h], k_ref[:, head(h)]), seen)
+        wt_x[h] = weight
+        sl_x[h] = slope
+
+    def cross_key(h):
+        da_copy[h].wait_recv()
+        grad_scores = (dot_nt(oda[h], v_ref[:, head(h)]) * sl_x[h]).astype(BF16)
+        dk_ref[:, head(h)] += dot_tn(grad_scores, oq[h]) * factor
+        dv_ref[:, head(h)] += dot_tn(wt_x[h], oda[h])
+
+    backward(0)
+    after_core(0)
+    backward(1)
+    after_core(1)
+    backward(2)
+    backward(3)
+    after_y(0)
+
+    @pl.when(ctx == 0)
+    def _():
+        for h in range(HEADS):
+            cross_scores(h)
+
+    @pl.when(ctx == 1)
+    def _():
+        for h in range(HEADS):
+            cross_query(h)
+
+    after_y(1)
+    after_z(0)
+    after_z(1)
+
+    @pl.when(ctx == 0)
+    def _():
+        for h in range(HEADS):
+            cross_key(h)
+        for h in range(HEADS):
+            k_copy[h].wait_send()
+            v_copy[h].wait_send()
+
+    @pl.when(ctx == 1)
+    def _():
+        for h in range(HEADS):
+            q_copy[h].wait_send()
+            da_copy[h].wait_send()
+
+    x_copy.wait_recv()
+    dw_ref[...] = fin[...] + r_x[...].astype(F32)
+    for copy in [stat_copy, w_copy, x_copy] + w_spread + c_copy + y_copy + z_copy[0] + z_copy[1]:
+        copy.wait_send()
+
+
+def fused(
+    users, queries, key_rows, value_rows, gate_rows, item_emb, labels, propensity, requests, lengths, w_out
+):
+    _, rows, feats = queries.shape
+    width = item_emb.shape[2]
+    per_user = width // users
+    nz = users // 4
+    cols = feats // 2
+    dma = pltpu.SemaphoreType.DMA
+    block = (HEADS, rows, HEAD_DIM)
+    square = (HEADS, rows, rows)
+    vmem = pl.BlockSpec(memory_space=pltpu.VMEM)
+    out = jax.ShapeDtypeStruct((rows, feats), F32)
+    results = pl.pallas_call(
+        functools.partial(fused_kernel, users),
+        out_shape=[out, out, out, out, jax.ShapeDtypeStruct((per_user, cols), F32)],
+        in_specs=[pl.BlockSpec(memory_space=pltpu.SMEM)] + [vmem] * 9,
+        out_specs=[vmem] * 5,
+        scratch_shapes=[
+            pltpu.VMEM(block, BF16),
+            pltpu.VMEM(block, BF16),
+            pltpu.VMEM(block, BF16),
+            pltpu.VMEM(block, BF16),
+            pltpu.VMEM((4, feats // 4, width // 2), BF16),
+            pltpu.VMEM((REQS, 128), F32),
+            pltpu.VMEM((REQS, 128), F32),
+            pltpu.VMEM(square, BF16),
+            pltpu.VMEM(square, F32),
+            pltpu.VMEM(square, BF16),
+            pltpu.VMEM(square, F32),
+            pltpu.VMEM((rows, feats), F32),
+            pltpu.VMEM((rows, feats), F32),
+            pltpu.VMEM(block, BF16),
+            pltpu.VMEM((2, 2, 2, nz, per_user, cols), BF16),
+            pltpu.VMEM((2, 2, nz, per_user, cols), BF16),
+            pltpu.VMEM((2, nz, per_user, cols), BF16),
+            pltpu.VMEM((2, nz, per_user, cols), BF16),
+            pltpu.VMEM((2, nz, per_user, cols), BF16),
+            pltpu.VMEM((2, nz - 1, per_user, cols), BF16),
+            pltpu.VMEM((per_user, cols), F32),
+            pltpu.VMEM((per_user, cols), BF16),
+            pltpu.VMEM((per_user, cols), BF16),
+        ]
+        + [dma((HEADS,))] * 8
+        + [dma((4,))] * 2
+        + [dma] * 2
+        + [dma((2,))] * 4
+        + [dma((2, nz - 1))] * 2
+        + [dma] * 2,
+        compiler_params=pltpu.CompilerParams(
+            collective_id=0, has_side_effects=True, vmem_limit_bytes=48 * 1024 * 1024
+        ),
+        cost_estimate=pl.CostEstimate(
+            flops=4 * 10**9, bytes_accessed=5 * 10**6, transcendentals=10**6
+        ),
+    )(
+        lengths, queries[0], key_rows[0], value_rows[0], gate_rows[0], item_emb[0],
+        labels, propensity, requests, w_out,
+    )
+    dq, dk, dv, dgate, dw = results
+    return dq[None], dk[None], dv[None], dgate[None], dw.T
+
+
 def solution(mesh):
     in_specs = (
         P("user", "ctx", None),
@@ -168,4 +526,7 @@
         P("user", "ctx", None),
         P("ctx", "user"),
     )
-    return jax.shard_map(local, mesh=mesh, in_specs=in_specs, out_specs=out_specs, check_vma=False)
+    users = mesh.shape["user"]
+    two_blocks = mesh.shape["ctx"] == 2 and users % 4 == 0
+    step = functools.partial(fused, users) if two_blocks else local
+    return jax.shard_map(step, mesh=mesh, in_specs=in_specs, out_specs=out_specs, check_vma=False)

time: 138 us -> 49 us (0.36)
  blocking collectives: 43.8 us -> 0 us
  waiting for transfers between devices: 42.4 us -> 0 us
  Pallas kernels: 0 us -> 37 us
  matrix products: 18.3 us -> 0 us
  between operations: 14.7 us -> 1.32 us
  other arithmetic: 5.75 us -> 0 us
  local copies, waits for them, and re-layouts: 12.7 us -> 10.4 us
    reduce_scatter x2 -> x0, waiting for transfers between devices: 41.7 us -> none  [the longest x1 31.5 us: local(): lax.psum_scatter(whole_grad, 'user', scatter_dimension=1, tiled=True)]
    all_gather x4 -> x0, blocking collectives: 38.9 us -> none  [the longest x1 14.8 us: local(): value_piece = lax.all_gather(own_value, 'ctx', axis=0, tiled=True)]
    pallas_call x0 -> x1, Pallas kernels: none -> 37 us  [fused(): pl.pallas_call(functools.partial(fused_kernel, users), out_shape=[out, ou...]
    dot_general x9 -> x0, matrix products: 18.3 us -> none  [the longest x1 3.39 us: local(): jnp.einsum('hqk,khd->qhd', grad_scores, key_piece_h, preferred_element_ty...]
    psum x1 -> x0, blocking collectives: 4.94 us -> none  [local(): lax.psum((jnp.sum(onehot * inv_prop[:, None], axis=0), jnp.sum(onehot * l...]
    unnamed x53 -> x23, local copies, waits for them, and re-layouts: 6.56 us -> 10.4 us
    another operation x3 -> x0, local copies, waits for them, and re-layouts: 2.01 us -> none  [split_heads(): return block.reshape(block.shape[0], HEADS, HEAD_DIM)]
    reshape x2 -> x0, local copies, waits for them, and re-layouts: 2 us -> none  [the longest x1 1 us: split_heads(): return block.reshape(block.shape[0], HEADS, HEAD_DIM)]
  transfers between devices with their start and end apart: 3 -> 0, of which waited for: 2 -> 0; matrix products, arithmetic and copies ran while one was open for 22% -> 0% of each run, Pallas kernels for 0% -> 0%
where the time goes in v1:
time: 49 us; the launch traced here: 48.7 us
  Pallas kernels  37 us (76%)
  local copies, waits for them, and re-layouts  10.4 us (21%)
  between operations  1.32 us (3%)
    pallas_call x1, Pallas kernels, fused(): pl.pallas_call(functools.partial(fused_kernel, users), out_shape=[out, ou...  37 us
    unnamed x23, local copies, waits for them, and re-layouts  10.4 us

profile of v1, /device:TPU:0, one launch (start us, length us, event | category | flops | bytes accessed | tf_op | source)
XLA Modules:
  0.0 48.7 jit_solution(13898974541103792417)
XLA Ops:
  1.3 0.0 copy-start.7
  1.3 0.0 copy-start.8
  1.3 0.0 copy-start.6
  1.3 0.7 %copy-done.7 = f32[1,256]{1,0:T(1,128)S(1)} copy-done((f32[1,256]{1,0:T(1,128)S(1)}, f32[1,256]{1,0:T(1,128)}, u32[]{:S(2)}) %copy-start.7) | copy-done | bytes 1048
  2.0 0.0 copy-done.8
  2.0 0.0 copy-done.6
  2.0 0.0 copy-start
  2.0 1.0 %copy-done = bf16[1,256,1024]{2,1,0:T(8,128)(2,1)S(1)} copy-done((bf16[1,256,1024]{2,1,0:T(8,128)(2,1)S(1)}, bf16[1,256,1024]{2,1,0:T(8,128)(2,1)}, u32[]{:S(2)}) %copy-start) | copy-done | bytes 524312
  3.0 0.0 copy-start.1
  3.0 1.0 %copy-done.1 = bf16[512,512]{1,0:T(8,128)(2,1)S(1)} copy-done((bf16[512,512]{1,0:T(8,128)(2,1)S(1)}, bf16[512,512]{1,0:T(8,128)(2,1)}, u32[]{:S(2)}) %copy-start.1) | copy-done | bytes 524312
  4.1 0.0 copy-start.2
  4.1 0.9 %copy-done.2 = bf16[1,256,512]{2,1,0:T(8,128)(2,1)S(1)} copy-done((bf16[1,256,512]{2,1,0:T(8,128)(2,1)S(1)}, bf16[1,256,512]{2,1,0:T(8,128)(2,1)}, u32[]{:S(2)}) %copy-start.2) | copy-done | bytes 262168
  5.0 0.0 copy-start.3
  5.0 0.9 %copy-done.3 = bf16[1,256,512]{2,1,0:T(8,128)(2,1)S(1)} copy-done((bf16[1,256,512]{2,1,0:T(8,128)(2,1)S(1)}, bf16[1,256,512]{2,1,0:T(8,128)(2,1)}, u32[]{:S(2)}) %copy-start.3) | copy-done | bytes 262168
  6.0 0.0 copy-start.4
  6.0 0.9 %copy-done.4 = bf16[1,256,512]{2,1,0:T(8,128)(2,1)S(1)} copy-done((bf16[1,256,512]{2,1,0:T(8,128)(2,1)S(1)}, bf16[1,256,512]{2,1,0:T(8,128)(2,1)}, u32[]{:S(2)}) %copy-start.4) | copy-done | bytes 262168
  6.9 0.0 copy-start.5
  6.9 0.9 %copy-done.5 = bf16[1,256,512]{2,1,0:T(8,128)(2,1)S(1)} copy-done((bf16[1,256,512]{2,1,0:T(8,128)(2,1)S(1)}, bf16[1,256,512]{2,1,0:T(8,128)(2,1)}, u32[]{:S(2)}) %copy-start.5) | copy-done | bytes 262168
  7.9 37.0 %shard_map.137 = (f32[256,512]{1,0:T(8,128)S(1)}, f32[256,512]{1,0:T(8,128)S(1)}, f32[256,512]{1,0:T(8,128)S(1)}, f32[256,512]{1,0:T(8,128)S(1)}, f32[64,256]{1,0:T(8,128)S(1)}) custom-call(s32[1]{0:T(128)S(6)} %copy.20.len_ref, bf16[256,512]{1,0:T(8,128)(2,1)S(1)} %bitcast.16, bf16[256,512]{1,0:T(8,128)(2,1)S(1)} %bitcast.17, ...), custom_call_target="tpu_custom_call" | custom-call | flops 4000000000 | bytes 5000000 | tf_op jit(solution)/shard_map/pallas_call | solution.py:459
  44.9 0.8 %copy.21 = f32[1,256,512]{2,1,0:T(8,128)} copy(f32[1,256,512]{2,1,0:T(8,128)S(1)} %bitcast.13) | data formatting | bytes 1048576
  45.7 0.8 %copy.22 = f32[1,256,512]{2,1,0:T(8,128)} copy(f32[1,256,512]{2,1,0:T(8,128)S(1)} %bitcast.12) | data formatting | bytes 1048576
  46.4 0.8 %copy.23 = f32[1,256,512]{2,1,0:T(8,128)} copy(f32[1,256,512]{2,1,0:T(8,128)S(1)} %bitcast.11) | data formatting | bytes 1048576
  47.2 0.8 %copy.24 = f32[1,256,512]{2,1,0:T(8,128)} copy(f32[1,256,512]{2,1,0:T(8,128)S(1)} %bitcast.10) | data formatting | bytes 1048576
  48.0 0.6 %copy.25 = f32[256,64]{0,1:T(8,128)} copy(f32[256,64]{0,1:T(8,128)S(1)} %bitcast.14) | data formatting | bytes 131072
Async XLA Ops:
  1.3 0.7 %copy-start.7 = (f32[1,256]{1,0:T(1,128)S(1)}, f32[1,256]{1,0:T(1,128)}, u32[]{:S(2)}) copy-start(f32[1,256]{1,0:T(1,128)} %prop_ref.1) | copy-start | bytes 3076
  1.3 0.7 %copy-start.8 = (s32[1,256]{1,0:T(1,128)S(1)}, s32[1,256]{1,0:T(1,128)}, u32[]{:S(2)}) copy-start(s32[1,256]{1,0:T(1,128)} %req_ref.1) | copy-start | bytes 3076
  1.3 0.7 %copy-start.6 = (s32[1,256]{1,0:T(1,128)S(1)}, s32[1,256]{1,0:T(1,128)}, u32[]{:S(2)}) copy-start(s32[1,256]{1,0:T(1,128)} %lab_ref.1) | copy-start | bytes 3076
  2.0 1.0 %copy-start = (bf16[1,256,1024]{2,1,0:T(8,128)(2,1)S(1)}, bf16[1,256,1024]{2,1,0:T(8,128)(2,1)}, u32[]{:S(2)}) copy-start(bf16[1,256,1024]{2,1,0:T(8,128)(2,1)} %param.14) | copy-start | bytes 1572868
  3.0 1.0 %copy-start.1 = (bf16[512,512]{1,0:T(8,128)(2,1)S(1)}, bf16[512,512]{1,0:T(8,128)(2,1)}, u32[]{:S(2)}) copy-start(bf16[512,512]{1,0:T(8,128)(2,1)} %w_ref.1) | copy-start | bytes 1572868
  4.1 0.9 %copy-start.2 = (bf16[1,256,512]{2,1,0:T(8,128)(2,1)S(1)}, bf16[1,256,512]{2,1,0:T(8,128)(2,1)}, u32[]{:S(2)}) copy-start(bf16[1,256,512]{2,1,0:T(8,128)(2,1)} %param.10) | copy-start | bytes 786436
  5.0 0.9 %copy-start.3 = (bf16[1,256,512]{2,1,0:T(8,128)(2,1)S(1)}, bf16[1,256,512]{2,1,0:T(8,128)(2,1)}, u32[]{:S(2)}) copy-start(bf16[1,256,512]{2,1,0:T(8,128)(2,1)} %param.11) | copy-start | bytes 786436
  6.0 0.9 %copy-start.4 = (bf16[1,256,512]{2,1,0:T(8,128)(2,1)S(1)}, bf16[1,256,512]{2,1,0:T(8,128)(2,1)}, u32[]{:S(2)}) copy-start(bf16[1,256,512]{2,1,0:T(8,128)(2,1)} %param.12) | copy-start | bytes 786436
  6.9 0.9 %copy-start.5 = (bf16[1,256,512]{2,1,0:T(8,128)(2,1)S(1)}, bf16[1,256,512]{2,1,0:T(8,128)(2,1)}, u32[]{:S(2)}) copy-start(bf16[1,256,512]{2,1,0:T(8,128)(2,1)} %param.13) | copy-start | bytes 786436

commit v2 on v1

--- a/solution.py
+++ b/solution.py
@@ -154,6 +154,7 @@
 MESH = pl.DeviceIdType.MESH
 F32 = jnp.float32
 BF16 = jnp.bfloat16
+NEAR = 2
 
 
 def dot_nn(a, b):
@@ -178,14 +179,22 @@
 
 def fused_kernel(
     users,
-    len_ref, q_ref, k_ref, v_ref, gate_ref, item_ref, lab_ref, prop_ref, req_ref, w_ref,
+    len_ref, q_hbm, k_hbm, v_hbm, gate_hbm, item_hbm, lab_hbm, prop_hbm, req_hbm, w_hbm,
     dq_ref, dk_ref, dv_ref, dgate_ref, dw_ref,
-    ok, ov, oq, oda, wbuf, stat_out, stat_in,
+    q_ref, k_ref, v_ref, gate_ref, item_ref, lab_ref, prop_ref, req_ref, w_ref, load,
+    ok, ov, oq, oda, wbuf, stat_out, stat_in, part_out, part_in, mixed, grad_proj_t,
     wt, sl, wt_x, sl_x, att, u, da, gw,
     r_core, s_y, r_y, s_z, r_z, fin, s_x, r_x,
-    ks, kr, vs, vr, qs, qr, das, dar, wss, wsr, sts, str_, cs, cr, ys, yr, zs, zr, xs, xr,
+    ks, kr, vs, vr, qs, qr, das, dar, wss, wsr, sts, str_, ps, pr, cs, cr, ys, yr, zs, zr, xs, xr,
 ):
     rows, feats = q_ref.shape
+    pairs = (
+        (q_hbm, q_ref), (k_hbm, k_ref), (v_hbm, v_ref), (w_hbm, w_ref), (item_hbm, item_ref),
+        (gate_hbm, gate_ref), (prop_hbm, prop_ref), (req_hbm, req_ref), (lab_hbm, lab_ref),
+    )
+    loads = [pltpu.make_async_copy(a, b, load.at[i]) for i, (a, b) in enumerate(pairs)]
+    for copy in loads:
+        copy.start()
     width = item_ref.shape[1]
     half_w = width // 2
     seq_len = 2 * rows
@@ -202,7 +211,7 @@
     x_peer = (1 - ctx, user)
     c_peer = (ctx, user + 1 - 2 * core)
     y_peer = (ctx, user + 2 - 4 * yy)
-    d_peer = (ctx, user + 3 - 2 * core - 4 * yy)
+    pair_peer = (ctx, quarter + 4 * (zz + 1 - 2 * lax.rem(zz, 2)))
     z_peers = [(ctx, quarter + 4 * lax.rem(zz + step, nz)) for step in range(1, nz)]
 
     def remote(source, target, send_sem, recv_sem, device):
@@ -211,48 +220,58 @@
             device_id=device, device_id_type=MESH,
         )
 
+    peers = [x_peer, c_peer, y_peer] + z_peers
+    barrier = pltpu.get_barrier_semaphore()
+    for peer in peers:
+        pl.semaphore_signal(barrier, inc=1, device_id=peer, device_id_type=MESH)
+    pl.semaphore_wait(barrier, len(peers))
+
+    stat_copy = remote(stat_out, stat_in, sts, str_, x_peer)
+    w_part = feats // 4
+    w_slice = w_part // 2
+    w_at = pl.multiple_of(lax.rem(zz, 2) * w_slice, w_slice)
+    w_rows = pl.ds(pl.multiple_of(quarter * w_part, w_part) + w_at, w_slice)
+    w_piece = wbuf.at[quarter, pl.ds(w_at, w_slice)]
+    far = quarter + 2 - 4 * yy
+    w_copy = remote(w_hbm.at[w_rows], w_piece, wss.at[0], wsr.at[0], x_peer)
+    w_pair = remote(w_piece, w_piece, wss.at[1], wsr.at[1], pair_peer)
+    w_core = remote(wbuf.at[quarter], wbuf.at[quarter], wss.at[2], wsr.at[2], c_peer)
+    w_y = remote(wbuf.at[quarter], wbuf.at[quarter], wss.at[3], wsr.at[3], y_peer)
+    w_far = remote(wbuf.at[far], wbuf.at[far], wss.at[4], wsr.at[4], c_peer)
+    w_all = [w_copy, w_pair, w_core, w_y, w_far]
+    k_copy = [remote(k_hbm.at[:, head(h)], ok.at[h], ks.at[h], kr.at[h], x_peer) for h in range(HEADS)]
+    v_copy = [remote(v_hbm.at[:, head(h)], ov.at[h], vs.at[h], vr.at[h], x_peer) for h in range(HEADS)]
+    q_copy = [remote(q_hbm.at[:, head(h)], oq.at[h], qs.at[h], qr.at[h], x_peer) for h in range(HEADS)]
+    da_copy = [remote(da.at[h], oda.at[h], das.at[h], dar.at[h], x_peer) for h in range(HEADS)]
+
+    part_copy = [remote(part_out.at[i], part_in.at[i], ps.at[i], pr.at[i], x_peer) for i in range(HEADS - NEAR)]
+    w_copy.start()
+
+    @pl.when(ctx == 0)
+    def _():
+        for h in range(NEAR):
+            k_copy[h].start()
+            v_copy[h].start()
+
+    @pl.when(ctx == 1)
+    def _():
+        for h in list(range(NEAR, HEADS)) + list(range(NEAR)):
+            q_copy[h].start()
+
+    for copy in loads:
+        copy.wait()
     hist_len = len_ref[0]
     reqs = req_ref[...]
     onehot = (lax.broadcasted_iota(jnp.int32, (REQS, rows), 0) == reqs).astype(F32)
     live = offset + lax.broadcasted_iota(jnp.int32, (1, rows), 1) < hist_len
     inv_prop = jnp.where(live, 1.0 / prop_ref[...], 0.0)
-    own_inv = jnp.sum(onehot * inv_prop, axis=1, keepdims=True)
-    own_live = jnp.sum(onehot * jnp.where(live, 1.0, 0.0), axis=1, keepdims=True)
-    lane = lax.broadcasted_iota(jnp.int32, (REQS, 128), 1)
-    stat_out[...] = jnp.where(lane == 0, own_inv, own_live)
-
-    peers = [x_peer, c_peer, y_peer, d_peer] + z_peers
-    barrier = pltpu.get_barrier_semaphore()
-    for peer in peers:
-        pl.semaphore_signal(barrier, inc=1, device_id=peer, device_id_type=MESH)
-    pl.semaphore_wait(barrier, len(peers))
-
-    stat_copy = remote(stat_out, stat_in, sts, str_, x_peer)
-    w_part = feats // 4
-    w_rows = pl.ds(pl.multiple_of(quarter * w_part, w_part), w_part)
-    w_copy = remote(w_ref.at[w_rows], wbuf.at[quarter], wss.at[0], wsr.at[0], x_peer)
-    w_spread = [
-        remote(wbuf.at[quarter], wbuf.at[quarter], wss.at[i], wsr.at[i], peer)
-        for i, peer in ((1, c_peer), (2, y_peer), (3, d_peer))
-    ]
-    k_copy = [remote(k_ref.at[:, head(h)], ok.at[h], ks.at[h], kr.at[h], x_peer) for h in range(HEADS)]
-    v_copy = [remote(v_ref.at[:, head(h)], ov.at[h], vs.at[h], vr.at[h], x_peer) for h in range(HEADS)]
-    q_copy = [remote(q_ref.at[:, head(h)], oq.at[h], qs.at[h], qr.at[h], x_peer) for h in range(HEADS)]
-    da_copy = [remote(da.at[h], oda.at[h], das.at[h], dar.at[h], x_peer) for h in range(HEADS)]
+    live_f = jnp.where(live, 1.0, 0.0)
+    stat_out[0:1] = reqs.astype(F32)
+    stat_out[1:2] = inv_prop
+    stat_out[2:3] = live_f
+    stat_out[3:8] = jnp.zeros((5, rows), F32)
 
     stat_copy.start()
-    w_copy.start()
-
-    @pl.when(ctx == 0)
-    def _():
-        for h in range(HEADS):
-            k_copy[h].start()
-            v_copy[h].start()
-
-    @pl.when(ctx == 1)
-    def _():
-        for h in range(HEADS):
-            q_copy[h].start()
 
     def gates(scores, allowed):
         s = scores * factor
@@ -272,23 +291,52 @@
 
     own_cols = pl.ds(pl.multiple_of(ctx * half_w, half_w), half_w)
     other_cols = pl.ds(pl.multiple_of((1 - ctx) * half_w, half_w), half_w)
+    seen = lax.broadcasted_iota(jnp.int32, (rows, rows), 1) < hist_len
+
+    def cross_scores(h):
+        q_copy[h].wait_recv()
+        weight, slope = gates(dot_nt(oq[h], k_ref[:, head(h)]), seen)
+        wt_x[h] = weight
+        sl_x[h] = slope
+
     w_copy.wait_recv()
-    for copy in w_spread:
-        copy.start()
+    w_pair.start()
+
+    @pl.when(ctx == 0)
+    def _():
+        for h in range(NEAR, HEADS):
+            cross_scores(h)
+            part_out[h - NEAR] = dot_nn(wt_x[h], v_ref[:, head(h)]).astype(BF16)
+            part_copy[h - NEAR].start()
+        for h in range(NEAR, HEADS):
+            k_copy[h].start()
+            v_copy[h].start()
+
+    w_pair.wait_recv()
+    w_y.start()
+    w_core.start()
     u[...] = dot_nt(item_ref[:, own_cols], w_ref[...])
 
     @pl.when(ctx == 1)
     def _():
-        seen = lax.broadcasted_iota(jnp.int32, (rows, rows), 1) < hist_len
-        for h in range(HEADS):
+        for h in range(NEAR):
             k_copy[h].wait_recv()
             weight, slope = gates(dot_nt(q_ref[:, head(h)], ok[h]), seen)
             sl_x[h] = slope
             v_copy[h].wait_recv()
             att[:, head(h)] += dot_nn(weight, ov[h])
 
-    for copy in w_spread:
-        copy.wait_recv()
+    w_y.wait_recv()
+    w_far.start()
+
+    @pl.when(ctx == 1)
+    def _():
+        for h in range(NEAR, HEADS):
+            part_copy[h - NEAR].wait_recv()
+            att[:, head(h)] += part_in[h - NEAR].astype(F32)
+
+    w_core.wait_recv()
+    w_far.wait_recv()
     for part in range(4):
         part_cols = slice(part * w_part, (part + 1) * w_part)
         u[:, part_cols] += dot_nt(item_ref[:, other_cols], wbuf[part])
@@ -303,8 +351,11 @@
     logits = jnp.sum(mixed_out.astype(F32) * item_proj, axis=-1, keepdims=True)
 
     stat_copy.wait_recv()
-    both = stat_out[...] + stat_in[...]
-    inv_sum, live_count = both[:, 0:1], both[:, 1:2]
+    onehot_x = (
+        lax.broadcasted_iota(jnp.int32, (REQS, rows), 0) == stat_in[0:1].astype(jnp.int32)
+    ).astype(F32)
+    inv_sum = jnp.sum(onehot * inv_prop + onehot_x * stat_in[1:2], axis=1, keepdims=True)
+    live_count = jnp.sum(onehot * live_f + onehot_x * stat_in[2:3], axis=1, keepdims=True)
     some = live_count > 0
     ratio = jnp.where(some, live_count / jnp.where(some, inv_sum, 1.0), 0.0)
     event_weight = inv_prop * jnp.sum(onehot * ratio, axis=0, keepdims=True)
@@ -329,17 +380,10 @@
             da_copy[h].start()
 
     per_user = width // users
-    for j in range(users // 2):
-        chunk_cols = slice(j * 2 * per_user, (j + 1) * 2 * per_user)
-        grad_proj = (grad_logits * item_ref[:, chunk_cols].astype(F32)).astype(BF16)
-        chunk = dot_tn(grad_proj, mixed_out).astype(BF16)
-        for c in range(2):
-            for half in range(2):
-                gw[c, half, j % 2, j // 2] = chunk[
-                    c * per_user : (c + 1) * per_user, half * cols : (half + 1) * cols
-                ]
+    for half in range(2):
+        mixed[half] = mixed_out[:, half * cols : (half + 1) * cols]
     halves = [1 - ctx, ctx]
-    c_copy = [remote(gw.at[1 - core, halves[o]], r_core.at[o], cs.at[o], cr.at[o], c_peer) for o in range(2)]
+    c_copy = [remote(gw.at[1 - core, o], r_core.at[o], cs.at[o], cr.at[o], c_peer) for o in range(2)]
     y_copy = [remote(s_y.at[o], r_y.at[o], ys.at[o], yr.at[o], y_peer) for o in range(2)]
     z_copy = [
         [
@@ -352,22 +396,30 @@
     ]
     x_copy = remote(s_x, r_x, xs, xr, x_peer)
     for o in range(2):
+        for j in range(users // 2):
+            if o == 0:
+                chunk_cols = slice(j * 2 * per_user, (j + 1) * 2 * per_user)
+                grad_proj = (grad_logits * item_ref[:, chunk_cols].astype(F32)).astype(BF16)
+                grad_proj_t[j] = grad_proj.T
+            chunk = dot_nn(grad_proj_t[j], mixed[halves[o]]).astype(BF16)
+            for c in range(2):
+                gw[c, o, j % 2, j // 2] = chunk[c * per_user : (c + 1) * per_user]
         c_copy[o].start()
 
     def after_core(o):
         c_copy[o].wait_recv()
-        s_y[o] = (gw[core, halves[o], 1 - yy].astype(F32) + r_core[o, 1 - yy].astype(F32)).astype(BF16)
+        s_y[o] = (gw[core, o, 1 - yy].astype(F32) + r_core[o, 1 - yy].astype(F32)).astype(BF16)
         y_copy[o].start()
 
     def after_y(o):
         y_copy[o].wait_recv()
-        mine = gw[core, halves[o], yy].astype(F32) + r_core[o, yy].astype(F32)
+        mine = gw[core, o, yy].astype(F32) + r_core[o, yy].astype(F32)
         s_z[o] = (mine + r_y[o].astype(F32)).astype(BF16)
         for copy in z_copy[o]:
             copy.start()
 
     def after_z(o):
-        total = gw[core, halves[o], yy, zz].astype(F32) + r_core[o, yy, zz].astype(F32)
+        total = gw[core, o, yy, zz].astype(F32) + r_core[o, yy, zz].astype(F32)
         total += r_y[o, zz].astype(F32)
         for i in range(nz - 1):
             z_copy[o][i].wait_recv()
@@ -388,13 +440,6 @@
         grad_scores = (dot_nt(da[h], ov[h]) * sl_x[h]).astype(BF16)
         dq_ref[:, head(h)] += dot_nn(grad_scores, ok[h]) * factor
 
-    def cross_scores(h):
-        q_copy[h].wait_recv()
-        seen = lax.broadcasted_iota(jnp.int32, (rows, rows), 1) < hist_len
-        weight, slope = gates(dot_nt(oq[h], k_ref[:, head(h)]), seen)
-        wt_x[h] = weight
-        sl_x[h] = slope
-
     def cross_key(h):
         da_copy[h].wait_recv()
         grad_scores = (dot_nt(oda[h], v_ref[:, head(h)]) * sl_x[h]).astype(BF16)
@@ -411,11 +456,15 @@
 
     @pl.when(ctx == 0)
     def _():
-        for h in range(HEADS):
+        for h in range(NEAR):
             cross_scores(h)
 
     @pl.when(ctx == 1)
     def _():
+        for h in range(NEAR, HEADS):
+            k_copy[h].wait_recv()
+            v_copy[h].wait_recv()
+            sl_x[h] = gates(dot_nt(q_ref[:, head(h)], ok[h]), seen)[1]
         for h in range(HEADS):
             cross_query(h)
 
@@ -430,6 +479,8 @@
         for h in range(HEADS):
             k_copy[h].wait_send()
             v_copy[h].wait_send()
+        for copy in part_copy:
+            copy.wait_send()
 
     @pl.when(ctx == 1)
     def _():
@@ -439,8 +490,19 @@
 
     x_copy.wait_recv()
     dw_ref[...] = fin[...] + r_x[...].astype(F32)
-    for copy in [stat_copy, w_copy, x_copy] + w_spread + c_copy + y_copy + z_copy[0] + z_copy[1]:
+    for copy in [stat_copy, x_copy] + w_all + c_copy + y_copy + z_copy[0] + z_copy[1]:
         copy.wait_send()
+
+
+def write_kernel(a, b, c, d, e, a_out, b_out, c_out, d_out, e_out, sems):
+    copies = [
+        pltpu.make_async_copy(src, dst, sems.at[i])
+        for i, (src, dst) in enumerate(((a, a_out), (b, b_out), (c, c_out), (d, d_out), (e, e_out)))
+    ]
+    for copy in copies:
+        copy.start()
+    for copy in copies:
+        copy.wait()
 
 
 def fused(
@@ -455,20 +517,40 @@
     block = (HEADS, rows, HEAD_DIM)
     square = (HEADS, rows, rows)
     vmem = pl.BlockSpec(memory_space=pltpu.VMEM)
+    hbm = pl.BlockSpec(memory_space=pltpu.HBM)
+    row = (1, rows)
     out = jax.ShapeDtypeStruct((rows, feats), F32)
+    operands = [
+        pltpu.with_memory_space_constraint(x, pltpu.HBM)
+        for x in (
+            queries[0], key_rows[0], value_rows[0], gate_rows[0], item_emb[0],
+            labels, propensity, requests, w_out,
+        )
+    ]
     results = pl.pallas_call(
         functools.partial(fused_kernel, users),
         out_shape=[out, out, out, out, jax.ShapeDtypeStruct((per_user, cols), F32)],
-        in_specs=[pl.BlockSpec(memory_space=pltpu.SMEM)] + [vmem] * 9,
+        in_specs=[pl.BlockSpec(memory_space=pltpu.SMEM)] + [hbm] * 9,
         out_specs=[vmem] * 5,
-        scratch_shapes=[
+        scratch_shapes=[pltpu.VMEM((rows, feats), BF16)] * 4
+        + [
+            pltpu.VMEM((rows, width), BF16),
+            pltpu.VMEM(row, jnp.int32),
+            pltpu.VMEM(row, F32),
+            pltpu.VMEM(row, jnp.int32),
+            pltpu.VMEM((feats, width // 2), BF16),
+            dma((9,)),
             pltpu.VMEM(block, BF16),
             pltpu.VMEM(block, BF16),
             pltpu.VMEM(block, BF16),
             pltpu.VMEM(block, BF16),
             pltpu.VMEM((4, feats // 4, width // 2), BF16),
-            pltpu.VMEM((REQS, 128), F32),
-            pltpu.VMEM((REQS, 128), F32),
+            pltpu.VMEM((8, rows), F32),
+            pltpu.VMEM((8, rows), F32),
+            pltpu.VMEM((HEADS - NEAR, rows, HEAD_DIM), BF16),
+            pltpu.VMEM((HEADS - NEAR, rows, HEAD_DIM), BF16),
+            pltpu.VMEM((2, rows, cols), BF16),
+            pltpu.VMEM((users // 2, 2 * per_user, rows), BF16),
             pltpu.VMEM(square, BF16),
             pltpu.VMEM(square, F32),
             pltpu.VMEM(square, BF16),
@@ -487,8 +569,9 @@
             pltpu.VMEM((per_user, cols), BF16),
         ]
         + [dma((HEADS,))] * 8
-        + [dma((4,))] * 2
+        + [dma((5,))] * 2
         + [dma] * 2
+        + [dma((HEADS - NEAR,))] * 2
         + [dma((2,))] * 4
         + [dma((2, nz - 1))] * 2
         + [dma] * 2,
@@ -498,11 +581,15 @@
         cost_estimate=pl.CostEstimate(
             flops=4 * 10**9, bytes_accessed=5 * 10**6, transcendentals=10**6
         ),
-    )(
-        lengths, queries[0], key_rows[0], value_rows[0], gate_rows[0], item_emb[0],
-        labels, propensity, requests, w_out,
-    )
-    dq, dk, dv, dgate, dw = results
+    )(lengths, *operands)
+    dq, dk, dv, dgate, dw = pl.pallas_call(
+        write_kernel,
+        out_shape=[jax.ShapeDtypeStruct(r.shape, F32) for r in results],
+        in_specs=[vmem] * 5,
+        out_specs=[hbm] * 5,
+        scratch_shapes=[dma((5,))],
+        cost_estimate=pl.CostEstimate(flops=0, bytes_accessed=2 * 10**6, transcendentals=0),
+    )(*results)
     return dq[None], dk[None], dv[None], dgate[None], dw.T
 
 
@@ -527,6 +614,6 @@
         P("ctx", "user"),
     )
     users = mesh.shape["user"]
-    two_blocks = mesh.shape["ctx"] == 2 and users % 4 == 0
+    two_blocks = mesh.shape["ctx"] == 2 and users % 8 == 0
     step = functools.partial(fused, users) if two_blocks else local
     return jax.shard_map(step, mesh=mesh, in_specs=in_specs, out_specs=out_specs, check_vma=False)

time: 49 us -> 43.5 us (0.89)
  local copies, waits for them, and re-layouts: 10.4 us -> 3.8 us
  Pallas kernels: 37 us -> 38.2 us
    unnamed x23 -> x10, local copies, waits for them, and re-layouts: 10.4 us -> 3.8 us
    pallas_call x0 -> x1, Pallas kernels: none -> 2.88 us  [fused(): pl.pallas_call(write_kernel, out_shape=[jax.ShapeDtypeStruct(r.shape, F32...]
    pallas_call x1, Pallas kernels: 37 us -> 35.3 us  [fused(): pl.pallas_call(functools.partial(fused_kernel, users), out_shape=[out, ou...]
where the time goes in v2:
time: 43.5 us; the launch traced here: 43.3 us
  Pallas kernels  38.2 us (88%)
  local copies, waits for them, and re-layouts  3.8 us (9%)
  between operations  1.3 us (3%)
    pallas_call x1, Pallas kernels, fused(): pl.pallas_call(functools.partial(fused_kernel, users), out_shape=[out, ou...  35.3 us
    unnamed x10, local copies, waits for them, and re-layouts  3.8 us
    pallas_call x1, Pallas kernels, fused(): pl.pallas_call(write_kernel, out_shape=[jax.ShapeDtypeStruct(r.shape, F32...  2.88 us

profile of v2, /device:TPU:0, one launch (start us, length us, event | category | flops | bytes accessed | tf_op | source)
XLA Modules:
  0.0 43.3 jit_solution(7432003146389662399)
XLA Ops:
  1.3 35.3 %shard_map.137 = (f32[256,512]{1,0:T(8,128)S(1)}, f32[256,512]{1,0:T(8,128)S(1)}, f32[256,512]{1,0:T(8,128)S(1)}, f32[256,512]{1,0:T(8,128)S(1)}, f32[64,256]{1,0:T(8,128)S(1)}) custom-call(s32[1]{0:T(128)S(6)} %copy.15.len_ref, bf16[256,512]{1,0:T(8,128)(2,1)} %bitcast.15, bf16[256,512]{1,0:T(8,128)(2,1)} %bitcast.16, bf16[256,512]{1,0:T(8,128)(2,1)} %bitcast.17, ...), custom_call_target="tpu_custom_call" | custom-call | flops 4000000000 | bytes 5000000 | tf_op jit(solution)/shard_map/pallas_call | solution.py:530
  36.6 0.0 copy-start
  36.6 0.8 %copy-done = f32[256,512]{1,0:T(8,128)} copy-done((f32[256,512]{1,0:T(8,128)}, f32[256,512]{1,0:T(8,128)S(1)}, u32[]{:S(2)}) %copy-start) | copy-done | bytes 524312
  37.4 0.0 copy-start.1
  37.4 0.8 %copy-done.1 = f32[256,512]{1,0:T(8,128)} copy-done((f32[256,512]{1,0:T(8,128)}, f32[256,512]{1,0:T(8,128)S(1)}, u32[]{:S(2)}) %copy-start.1) | copy-done | bytes 524312
  38.2 0.0 copy-start.2
  38.2 0.8 %copy-done.2 = f32[256,512]{1,0:T(8,128)} copy-done((f32[256,512]{1,0:T(8,128)}, f32[256,512]{1,0:T(8,128)S(1)}, u32[]{:S(2)}) %copy-start.2) | copy-done | bytes 524312
  39.0 0.0 copy-start.3
  39.0 0.8 %copy-done.3 = f32[256,512]{1,0:T(8,128)} copy-done((f32[256,512]{1,0:T(8,128)}, f32[256,512]{1,0:T(8,128)S(1)}, u32[]{:S(2)}) %copy-start.3) | copy-done | bytes 524312
  39.8 0.0 copy-start.4
  39.8 0.6 %copy-done.4 = f32[64,256]{1,0:T(8,128)} copy-done((f32[64,256]{1,0:T(8,128)}, f32[64,256]{1,0:T(8,128)S(1)}, u32[]{:S(2)}) %copy-start.4) | copy-done | bytes 65560
  40.4 2.9 %shard_map.138 = (f32[256,512]{1,0:T(8,128)}, f32[256,512]{1,0:T(8,128)}, f32[256,512]{1,0:T(8,128)}, f32[256,512]{1,0:T(8,128)}, f32[64,256]{1,0:T(8,128)}) custom-call(f32[256,512]{1,0:T(8,128)} %copy-done, f32[256,512]{1,0:T(8,128)} %copy-done.1, f32[256,512]{1,0:T(8,128)} %copy-done.2, f32[256,512]{1,0:T(8,128)} %copy-done.3, f32[64,256]{1,0:T(8,128)} %copy-done.4), custom_call_target="tpu_custom_call" | custom-call | bytes 2000000 | tf_op jit(solution)/shard_map/pallas_call | solution.py:585
Async XLA Ops:
  36.6 0.8 %copy-start = (f32[256,512]{1,0:T(8,128)}, f32[256,512]{1,0:T(8,128)S(1)}, u32[]{:S(2)}) copy-start(f32[256,512]{1,0:T(8,128)S(1)} %get-tuple-element.15.a) | copy-start | bytes 1572868
  37.4 0.8 %copy-start.1 = (f32[256,512]{1,0:T(8,128)}, f32[256,512]{1,0:T(8,128)S(1)}, u32[]{:S(2)}) copy-start(f32[256,512]{1,0:T(8,128)S(1)} %get-tuple-element.16.b) | copy-start | bytes 1572868
  38.2 0.8 %copy-start.2 = (f32[256,512]{1,0:T(8,128)}, f32[256,512]{1,0:T(8,128)S(1)}, u32[]{:S(2)}) copy-start(f32[256,512]{1,0:T(8,128)S(1)} %get-tuple-element.17.c) | copy-start | bytes 1572868
  39.0 0.8 %copy-start.3 = (f32[256,512]{1,0:T(8,128)}, f32[256,512]{1,0:T(8,128)S(1)}, u32[]{:S(2)}) copy-start(f32[256,512]{1,0:T(8,128)S(1)} %get-tuple-element.18.d) | copy-start | bytes 1572868
  39.8 0.6 %copy-start.4 = (f32[64,256]{1,0:T(8,128)}, f32[64,256]{1,0:T(8,128)S(1)}, u32[]{:S(2)}) copy-start(f32[64,256]{1,0:T(8,128)S(1)} %get-tuple-element.19.e) | copy-start | bytes 196612

commit v3 on v2

--- a/solution.py
+++ b/solution.py
@@ -155,6 +155,8 @@
 F32 = jnp.float32
 BF16 = jnp.bfloat16
 NEAR = 2
+W_FIRST = 1
+PIECES = 4
 
 
 def dot_nn(a, b):
@@ -182,7 +184,7 @@
     len_ref, q_hbm, k_hbm, v_hbm, gate_hbm, item_hbm, lab_hbm, prop_hbm, req_hbm, w_hbm,
     dq_ref, dk_ref, dv_ref, dgate_ref, dw_ref,
     q_ref, k_ref, v_ref, gate_ref, item_ref, lab_ref, prop_ref, req_ref, w_ref, load,
-    ok, ov, oq, oda, wbuf, stat_out, stat_in, part_out, part_in, mixed, grad_proj_t,
+    ok, ov, oq, oda, wbuf, stat_out, stat_in, part_out, part_in, mixed, item_t,
     wt, sl, wt_x, sl_x, att, u, da, gw,
     r_core, s_y, r_y, s_z, r_z, fin, s_x, r_x,
     ks, kr, vs, vr, qs, qr, das, dar, wss, wsr, sts, str_, ps, pr, cs, cr, ys, yr, zs, zr, xs, xr,
@@ -230,15 +232,20 @@
     w_part = feats // 4
     w_slice = w_part // 2
     w_at = pl.multiple_of(lax.rem(zz, 2) * w_slice, w_slice)
+    w_next = pl.multiple_of((1 - lax.rem(zz, 2)) * w_slice, w_slice)
     w_rows = pl.ds(pl.multiple_of(quarter * w_part, w_part) + w_at, w_slice)
-    w_piece = wbuf.at[quarter, pl.ds(w_at, w_slice)]
     far = quarter + 2 - 4 * yy
-    w_copy = remote(w_hbm.at[w_rows], w_piece, wss.at[0], wsr.at[0], x_peer)
-    w_pair = remote(w_piece, w_piece, wss.at[1], wsr.at[1], pair_peer)
-    w_core = remote(wbuf.at[quarter], wbuf.at[quarter], wss.at[2], wsr.at[2], c_peer)
-    w_y = remote(wbuf.at[quarter], wbuf.at[quarter], wss.at[3], wsr.at[3], y_peer)
-    w_far = remote(wbuf.at[far], wbuf.at[far], wss.at[4], wsr.at[4], c_peer)
-    w_all = [w_copy, w_pair, w_core, w_y, w_far]
+
+    def spread(i, quarter_at, row_at, peer):
+        rows_at = wbuf.at[quarter_at, pl.ds(row_at, w_slice)]
+        return remote(rows_at, rows_at, wss.at[i], wsr.at[i], peer)
+
+    w_copy = remote(w_hbm.at[w_rows], wbuf.at[quarter, pl.ds(w_at, w_slice)], wss.at[0], wsr.at[0], x_peer)
+    w_pair = spread(1, quarter, w_at, pair_peer)
+    w_y = [spread(2, quarter, w_at, y_peer), spread(3, quarter, w_next, y_peer)]
+    w_core = [spread(4, quarter, w_at, c_peer), spread(5, quarter, w_next, c_peer)]
+    w_far = [spread(6, far, w_at, c_peer), spread(7, far, w_next, c_peer)]
+    w_all = [w_copy, w_pair] + w_y + w_core + w_far
     k_copy = [remote(k_hbm.at[:, head(h)], ok.at[h], ks.at[h], kr.at[h], x_peer) for h in range(HEADS)]
     v_copy = [remote(v_hbm.at[:, head(h)], ov.at[h], vs.at[h], vr.at[h], x_peer) for h in range(HEADS)]
     q_copy = [remote(q_hbm.at[:, head(h)], oq.at[h], qs.at[h], qr.at[h], x_peer) for h in range(HEADS)]
@@ -255,7 +262,9 @@
 
     @pl.when(ctx == 1)
     def _():
-        for h in list(range(NEAR, HEADS)) + list(range(NEAR)):
+        for h in range(NEAR, HEADS):
+            q_copy[h].start()
+        for h in range(NEAR):
             q_copy[h].start()
 
     for copy in loads:
@@ -288,6 +297,15 @@
         wt[h] = weight
         sl[h] = slope
         att[:, head(h)] = dot_nn(weight, v_ref[:, head(h)])
+        if h == W_FIRST:
+            w_copy.wait_recv()
+            w_pair.start()
+            w_y[0].start()
+            w_core[0].start()
+
+    w_pair.wait_recv()
+    w_y[1].start()
+    w_core[1].start()
 
     own_cols = pl.ds(pl.multiple_of(ctx * half_w, half_w), half_w)
     other_cols = pl.ds(pl.multiple_of((1 - ctx) * half_w, half_w), half_w)
@@ -298,9 +316,6 @@
         weight, slope = gates(dot_nt(oq[h], k_ref[:, head(h)]), seen)
         wt_x[h] = weight
         sl_x[h] = slope
-
-    w_copy.wait_recv()
-    w_pair.start()
 
     @pl.when(ctx == 0)
     def _():
@@ -312,31 +327,38 @@
             k_copy[h].start()
             v_copy[h].start()
 
-    w_pair.wait_recv()
-    w_y.start()
-    w_core.start()
     u[...] = dot_nt(item_ref[:, own_cols], w_ref[...])
+    per_user = width // users
+    for j in range(users // 2):
+        item_t[j] = item_ref[:, j * 2 * per_user : (j + 1) * 2 * per_user].T
+
+    w_y[0].wait_recv()
+    w_far[0].start()
+
+    def look_back(h):
+        k_copy[h].wait_recv()
+        weight, slope = gates(dot_nt(q_ref[:, head(h)], ok[h]), seen)
+        sl_x[h] = slope
+        v_copy[h].wait_recv()
+        att[:, head(h)] += dot_nn(weight, ov[h])
 
     @pl.when(ctx == 1)
     def _():
-        for h in range(NEAR):
-            k_copy[h].wait_recv()
-            weight, slope = gates(dot_nt(q_ref[:, head(h)], ok[h]), seen)
-            sl_x[h] = slope
-            v_copy[h].wait_recv()
-            att[:, head(h)] += dot_nn(weight, ov[h])
-
-    w_y.wait_recv()
-    w_far.start()
+        look_back(0)
+
+    w_y[1].wait_recv()
+    w_far[1].start()
 
     @pl.when(ctx == 1)
     def _():
+        for h in range(1, NEAR):
+            look_back(h)
         for h in range(NEAR, HEADS):
             part_copy[h - NEAR].wait_recv()
             att[:, head(h)] += part_in[h - NEAR].astype(F32)
 
-    w_core.wait_recv()
-    w_far.wait_recv()
+    for copy in w_core + w_far:
+        copy.wait_recv()
     for part in range(4):
         part_cols = slice(part * w_part, (part + 1) * w_part)
         u[:, part_cols] += dot_nt(item_ref[:, other_cols], wbuf[part])
@@ -363,6 +385,36 @@
     weight_col = jnp.sum(jnp.where(eye, event_weight, 0.0), axis=1, keepdims=True)
     label_col = jnp.sum(jnp.where(eye, lab_ref[...].astype(F32), 0.0), axis=1, keepdims=True)
     grad_logits = weight_col * (jax.nn.sigmoid(logits) - label_col)
+    weighted = (grad_logits * mixed_out.astype(F32)).astype(BF16)
+    for half in range(2):
+        mixed[half] = weighted[:, half * cols : (half + 1) * cols]
+    halves = [1 - ctx, ctx]
+    piece = feats // PIECES
+    c_copy = [remote(gw.at[1 - core, o], r_core.at[o], cs.at[o], cr.at[o], c_peer) for o in range(PIECES)]
+    y_copy = [remote(s_y.at[o], r_y.at[o], ys.at[o], yr.at[o], y_peer) for o in range(PIECES)]
+    z_copy = [
+        [
+            remote(
+                s_z.at[o, lax.rem(zz + i + 1, nz)], r_z.at[o, i], zs.at[o, i], zr.at[o, i], z_peers[i]
+            )
+            for i in range(nz - 1)
+        ]
+        for o in range(PIECES)
+    ]
+    x_copy = [remote(s_x.at[o], r_x.at[o], xs.at[o], xr.at[o], x_peer) for o in range(PIECES // 2)]
+    def weight_grad(o):
+        for j in range(users // 2):
+            chunk = dot_nn(item_t[j], mixed[halves[o]]).astype(BF16)
+            for c in range(2):
+                for p in range(PIECES // 2):
+                    gw[c, o * PIECES // 2 + p, j % 2, j // 2] = chunk[
+                        c * per_user : (c + 1) * per_user, p * piece : (p + 1) * piece
+                    ]
+        for p in range(PIECES // 2):
+            c_copy[o * PIECES // 2 + p].start()
+
+    weight_grad(0)
+    weight_grad(1)
     grad_mixed = grad_logits * item_proj
     dgate_ref[...] = grad_mixed * normed
     grad_normed = grad_mixed * gate_f
@@ -379,33 +431,6 @@
         for h in range(HEADS):
             da_copy[h].start()
 
-    per_user = width // users
-    for half in range(2):
-        mixed[half] = mixed_out[:, half * cols : (half + 1) * cols]
-    halves = [1 - ctx, ctx]
-    c_copy = [remote(gw.at[1 - core, o], r_core.at[o], cs.at[o], cr.at[o], c_peer) for o in range(2)]
-    y_copy = [remote(s_y.at[o], r_y.at[o], ys.at[o], yr.at[o], y_peer) for o in range(2)]
-    z_copy = [
-        [
-            remote(
-                s_z.at[o, lax.rem(zz + i + 1, nz)], r_z.at[o, i], zs.at[o, i], zr.at[o, i], z_peers[i]
-            )
-            for i in range(nz - 1)
-        ]
-        for o in range(2)
-    ]
-    x_copy = remote(s_x, r_x, xs, xr, x_peer)
-    for o in range(2):
-        for j in range(users // 2):
-            if o == 0:
-                chunk_cols = slice(j * 2 * per_user, (j + 1) * 2 * per_user)
-                grad_proj = (grad_logits * item_ref[:, chunk_cols].astype(F32)).astype(BF16)
-                grad_proj_t[j] = grad_proj.T
-            chunk = dot_nn(grad_proj_t[j], mixed[halves[o]]).astype(BF16)
-            for c in range(2):
-                gw[c, o, j % 2, j // 2] = chunk[c * per_user : (c + 1) * per_user]
-        c_copy[o].start()
-
     def after_core(o):
         c_copy[o].wait_recv()
         s_y[o] = (gw[core, o, 1 - yy].astype(F32) + r_core[o, 1 - yy].astype(F32)).astype(BF16)
@@ -424,11 +449,11 @@
         for i in range(nz - 1):
             z_copy[o][i].wait_recv()
             total += r_z[o, i].astype(F32)
-        if o == 0:
-            s_x[...] = total.astype(BF16)
-            x_copy.start()
+        if o < PIECES // 2:
+            s_x[o] = total.astype(BF16)
+            x_copy[o].start()
         else:
-            fin[...] = total
+            fin[o - PIECES // 2] = total
 
     def backward(h):
         grad_scores = (dot_nt(da[h], v_ref[:, head(h)]) * sl[h]).astype(BF16)
@@ -446,18 +471,24 @@
         dk_ref[:, head(h)] += dot_tn(grad_scores, oq[h]) * factor
         dv_ref[:, head(h)] += dot_tn(wt_x[h], oda[h])
 
-    backward(0)
-    after_core(0)
-    backward(1)
-    after_core(1)
-    backward(2)
-    backward(3)
-    after_y(0)
+    for o in range(PIECES):
+        after_core(o)
+    for h in range(HEADS):
+        backward(h)
+        if h > 0:
+            after_y(h - 1)
 
     @pl.when(ctx == 0)
     def _():
         for h in range(NEAR):
             cross_scores(h)
+
+    @pl.when(ctx == 1)
+    def _():
+        for h in range(NEAR):
+            cross_query(h)
+
+    after_y(3)
 
     @pl.when(ctx == 1)
     def _():
@@ -465,12 +496,10 @@
             k_copy[h].wait_recv()
             v_copy[h].wait_recv()
             sl_x[h] = gates(dot_nt(q_ref[:, head(h)], ok[h]), seen)[1]
-        for h in range(HEADS):
             cross_query(h)
 
-    after_y(1)
-    after_z(0)
-    after_z(1)
+    for o in range(PIECES):
+        after_z(o)
 
     @pl.when(ctx == 0)
     def _():
@@ -488,9 +517,10 @@
             q_copy[h].wait_send()
             da_copy[h].wait_send()
 
-    x_copy.wait_recv()
-    dw_ref[...] = fin[...] + r_x[...].astype(F32)
-    for copy in [stat_copy, x_copy] + w_all + c_copy + y_copy + z_copy[0] + z_copy[1]:
+    for o in range(PIECES // 2):
+        x_copy[o].wait_recv()
+        dw_ref[:, o * piece : (o + 1) * piece] = fin[o] + r_x[o].astype(F32)
+    for copy in [stat_copy] + x_copy + w_all + c_copy + y_copy + sum(z_copy, []):
         copy.wait_send()
 
 
@@ -513,6 +543,7 @@
     per_user = width // users
     nz = users // 4
     cols = feats // 2
+    piece = feats // PIECES
     dma = pltpu.SemaphoreType.DMA
     block = (HEADS, rows, HEAD_DIM)
     square = (HEADS, rows, rows)
@@ -558,23 +589,23 @@
             pltpu.VMEM((rows, feats), F32),
             pltpu.VMEM((rows, feats), F32),
             pltpu.VMEM(block, BF16),
-            pltpu.VMEM((2, 2, 2, nz, per_user, cols), BF16),
-            pltpu.VMEM((2, 2, nz, per_user, cols), BF16),
-            pltpu.VMEM((2, nz, per_user, cols), BF16),
-            pltpu.VMEM((2, nz, per_user, cols), BF16),
-            pltpu.VMEM((2, nz, per_user, cols), BF16),
-            pltpu.VMEM((2, nz - 1, per_user, cols), BF16),
-            pltpu.VMEM((per_user, cols), F32),
-            pltpu.VMEM((per_user, cols), BF16),
-            pltpu.VMEM((per_user, cols), BF16),
+            pltpu.VMEM((2, PIECES, 2, nz, per_user, piece), BF16),
+            pltpu.VMEM((PIECES, 2, nz, per_user, piece), BF16),
+            pltpu.VMEM((PIECES, nz, per_user, piece), BF16),
+            pltpu.VMEM((PIECES, nz, per_user, piece), BF16),
+            pltpu.VMEM((PIECES, nz, per_user, piece), BF16),
+            pltpu.VMEM((PIECES, nz - 1, per_user, piece), BF16),
+            pltpu.VMEM((PIECES // 2, per_user, piece), F32),
+            pltpu.VMEM((PIECES // 2, per_user, piece), BF16),
+            pltpu.VMEM((PIECES // 2, per_user, piece), BF16),
         ]
         + [dma((HEADS,))] * 8
-        + [dma((5,))] * 2
+        + [dma((8,))] * 2
         + [dma] * 2
         + [dma((HEADS - NEAR,))] * 2
-        + [dma((2,))] * 4
-        + [dma((2, nz - 1))] * 2
-        + [dma] * 2,
+        + [dma((PIECES,))] * 4
+        + [dma((PIECES, nz - 1))] * 2
+        + [dma((PIECES // 2,))] * 2,
         compiler_params=pltpu.CompilerParams(
             collective_id=0, has_side_effects=True, vmem_limit_bytes=48 * 1024 * 1024
         ),
@@ -588,8 +619,9 @@
         in_specs=[vmem] * 5,
         out_specs=[hbm] * 5,
         scratch_shapes=[dma((5,))],
+        compiler_params=pltpu.CompilerParams(vmem_limit_bytes=4 * 1024 * 1024),
         cost_estimate=pl.CostEstimate(flops=0, bytes_accessed=2 * 10**6, transcendentals=0),
-    )(*results)
+    )(*[pltpu.with_memory_space_constraint(r, pltpu.VMEM) for r in results])
     return dq[None], dk[None], dv[None], dgate[None], dw.T
 
 

time: 43.5 us -> 36.2 us (0.83)
  local copies, waits for them, and re-layouts: 3.8 us -> 0 us
  Pallas kernels: 38.2 us -> 34.7 us
    unnamed x10 -> x0, local copies, waits for them, and re-layouts: 3.8 us -> none
    pallas_call x1, Pallas kernels: 35.3 us -> 33.4 us  [fused(): pl.pallas_call(functools.partial(fused_kernel, users), out_shape=[out, ou...]
    pallas_call x1, Pallas kernels: 2.88 us -> 1.37 us  [fused(): pl.pallas_call(write_kernel, out_shape=[jax.ShapeDtypeStruct(r.shape, F32...]
where the time goes in v3:
time: 36.2 us; the launch traced here: 36 us
  Pallas kernels  34.7 us (96%)
  between operations  1.29 us (4%)
    pallas_call x1, Pallas kernels, fused(): pl.pallas_call(functools.partial(fused_kernel, users), out_shape=[out, ou...  33.4 us
    pallas_call x1, Pallas kernels, fused(): pl.pallas_call(write_kernel, out_shape=[jax.ShapeDtypeStruct(r.shape, F32...  1.37 us

profile of v3, /device:TPU:0, one launch (start us, length us, event | category | flops | bytes accessed | tf_op | source)
XLA Modules:
  0.0 36.0 jit_solution(8975482001459805731)
XLA Ops:
  1.3 33.4 %shard_map.137 = (f32[256,512]{1,0:T(8,128)S(1)}, f32[256,512]{1,0:T(8,128)S(1)}, f32[256,512]{1,0:T(8,128)S(1)}, f32[256,512]{1,0:T(8,128)S(1)}, f32[64,256]{1,0:T(8,128)S(1)}) custom-call(s32[1]{0:T(128)S(6)} %copy.15.len_ref, bf16[256,512]{1,0:T(8,128)(2,1)} %bitcast.15, bf16[256,512]{1,0:T(8,128)(2,1)} %bitcast.16, bf16[256,512]{1,0:T(8,128)(2,1)} %bitcast.17, ...), custom_call_target="tpu_custom_call" | custom-call | flops 4000000000 | bytes 5000000 | tf_op jit(solution)/shard_map/pallas_call | solution.py:561
  34.7 1.4 %shard_map.138 = (f32[256,512]{1,0:T(8,128)}, f32[256,512]{1,0:T(8,128)}, f32[256,512]{1,0:T(8,128)}, f32[256,512]{1,0:T(8,128)}, f32[64,256]{1,0:T(8,128)}) custom-call(f32[256,512]{1,0:T(8,128)S(1)} %get-tuple-element.15.a, f32[256,512]{1,0:T(8,128)S(1)} %get-tuple-element.16.b, f32[256,512]{1,0:T(8,128)S(1)} %get-tuple-element.17.c, ...), custom_call_target="tpu_custom_call" | custom-call | bytes 2000000 | tf_op jit(solution)/shard_map/pallas_call | solution.py:616

commit v4 on v3

--- a/solution.py
+++ b/solution.py
@@ -415,21 +415,6 @@
 
     weight_grad(0)
     weight_grad(1)
-    grad_mixed = grad_logits * item_proj
-    dgate_ref[...] = grad_mixed * normed
-    grad_normed = grad_mixed * gate_f
-    grad_attn = (
-        grad_normed
-        - jnp.mean(grad_normed, axis=-1, keepdims=True)
-        - normed * jnp.mean(grad_normed * normed, axis=-1, keepdims=True)
-    ) * inv_std
-    for h in range(HEADS):
-        da[h] = grad_attn[:, head(h)].astype(BF16)
-
-    @pl.when(ctx == 1)
-    def _():
-        for h in range(HEADS):
-            da_copy[h].start()
 
     def after_core(o):
         c_copy[o].wait_recv()
@@ -473,6 +458,23 @@
 
     for o in range(PIECES):
         after_core(o)
+
+    grad_mixed = grad_logits * item_proj
+    dgate_ref[...] = grad_mixed * normed
+    grad_normed = grad_mixed * gate_f
+    grad_attn = (
+        grad_normed
+        - jnp.mean(grad_normed, axis=-1, keepdims=True)
+        - normed * jnp.mean(grad_normed * normed, axis=-1, keepdims=True)
+    ) * inv_std
+    for h in range(HEADS):
+        da[h] = grad_attn[:, head(h)].astype(BF16)
+
+    @pl.when(ctx == 1)
+    def _():
+        for h in range(HEADS):
+            da_copy[h].start()
+
     for h in range(HEADS):
         backward(h)
         if h > 0:
@@ -489,6 +491,9 @@
             cross_query(h)
 
     after_y(3)
+
+    for o in range(PIECES // 2):
+        after_z(o)
 
     @pl.when(ctx == 1)
     def _():
@@ -498,13 +503,16 @@
             sl_x[h] = gates(dot_nt(q_ref[:, head(h)], ok[h]), seen)[1]
             cross_query(h)
 
-    for o in range(PIECES):
-        after_z(o)
-
     @pl.when(ctx == 0)
     def _():
         for h in range(HEADS):
             cross_key(h)
+
+    for o in range(PIECES // 2, PIECES):
+        after_z(o)
+
+    @pl.when(ctx == 0)
+    def _():
         for h in range(HEADS):
             k_copy[h].wait_send()
             v_copy[h].wait_send()

time: 36.2 us -> 35.8 us (0.989)
  Pallas kernels: 34.7 us -> 34.3 us
    pallas_call x1, Pallas kernels: 33.4 us -> 33 us  [fused(): pl.pallas_call(functools.partial(fused_kernel, users), out_shape=[out, ou...]
where the time goes in v4:
time: 35.8 us; the launch traced here: 35.6 us
  Pallas kernels  34.3 us (96%)
  between operations  1.29 us (4%)
    pallas_call x1, Pallas kernels, fused(): pl.pallas_call(functools.partial(fused_kernel, users), out_shape=[out, ou...  33 us
    pallas_call x1, Pallas kernels, fused(): pl.pallas_call(write_kernel, out_shape=[jax.ShapeDtypeStruct(r.shape, F32...  1.37 us

profile of v4, /device:TPU:0, one launch (start us, length us, event | category | flops | bytes accessed | tf_op | source)
XLA Modules:
  0.0 35.6 jit_solution(3365211979426797019)
XLA Ops:
  1.3 33.0 %shard_map.137 = (f32[256,512]{1,0:T(8,128)S(1)}, f32[256,512]{1,0:T(8,128)S(1)}, f32[256,512]{1,0:T(8,128)S(1)}, f32[256,512]{1,0:T(8,128)S(1)}, f32[64,256]{1,0:T(8,128)S(1)}) custom-call(s32[1]{0:T(128)S(6)} %copy.15.len_ref, bf16[256,512]{1,0:T(8,128)(2,1)} %bitcast.15, bf16[256,512]{1,0:T(8,128)(2,1)} %bitcast.16, bf16[256,512]{1,0:T(8,128)(2,1)} %bitcast.17, ...), custom_call_target="tpu_custom_call" | custom-call | flops 4000000000 | bytes 5000000 | tf_op jit(solution)/shard_map/pallas_call | solution.py:569
  34.3 1.4 %shard_map.138 = (f32[256,512]{1,0:T(8,128)}, f32[256,512]{1,0:T(8,128)}, f32[256,512]{1,0:T(8,128)}, f32[256,512]{1,0:T(8,128)}, f32[64,256]{1,0:T(8,128)}) custom-call(f32[256,512]{1,0:T(8,128)S(1)} %get-tuple-element.15.a, f32[256,512]{1,0:T(8,128)S(1)} %get-tuple-element.16.b, f32[256,512]{1,0:T(8,128)S(1)} %get-tuple-element.17.c, ...), custom_call_target="tpu_custom_call" | custom-call | bytes 2000000 | tf_op jit(solution)/shard_map/pallas_call | solution.py:624
